TPU v7x, 32 devices: a whole 2x2x4 slice. The times are simulated.
32 devices in a mesh: dp: 16 (over z, y, x), mp: 2 (over core).
Axes of the slice: x: 2, y: 2, z: 4, core: 2. Of those that a mesh axis runs over, the one named last changes fastest.
Arguments:
- small_images: bfloat16 [64, 196, 768], P('dp', None, 'mp'), may hold values from -6 to 6
- large_images: bfloat16 [64, 576, 768], P('dp', None, 'mp'), may hold values from -6 to 6
- token_gain: float32 [768], P('mp'), may hold values from 0.5 to 1.5
- token_shift: float32 [768], P('mp'), may hold values from -1.75 to 1.75
- small_expand: bfloat16 [196, 384], replicated, may hold values from -0.4375 to 0.4375
- small_expand_bias: float32 [384], replicated, may hold values from -1.75 to 1.75
- small_project: bfloat16 [384, 196], replicated, may hold values from -0.3125 to 0.3125
- small_project_bias: float32 [196], replicated, may hold values from -1.75 to 1.75
- large_expand: bfloat16 [576, 384], replicated, may hold values from -0.25 to 0.25
- large_expand_bias: float32 [384], replicated, may hold values from -1.75 to 1.75
- large_project: bfloat16 [384, 576], replicated, may hold values from -0.3125 to 0.3125
- large_project_bias: float32 [576], replicated, may hold values from -1.75 to 1.75
- channel_gain: float32 [768], replicated, may hold values from 0.5 to 1.5
- channel_shift: float32 [768], replicated, may hold values from -1.75 to 1.75
- channel_expand: bfloat16 [768, 3072], replicated, may hold values from -0.21875 to 0.21875
- channel_expand_bias: float32 [3072], replicated, may hold values from -1.75 to 1.75
- channel_project: bfloat16 [3072, 768], replicated, may hold values from -0.109375 to 0.109375
- channel_project_bias: float32 [768], replicated, may hold values from -1.75 to 1.75
- small_cotangent: bfloat16 [64, 196, 768], P('dp', 'mp'), may hold values from -6 to 6
- large_cotangent: bfloat16 [64, 576, 768], P('dp', 'mp'), may hold values from -6 to 6
Outputs:
- small_output: bfloat16 [64, 196, 768], P('dp', 'mp')
- large_output: bfloat16 [64, 576, 768], P('dp', 'mp')
- small_input_grad: bfloat16 [64, 196, 768], P('dp', None, 'mp')
- large_input_grad: bfloat16 [64, 576, 768], P('dp', None, 'mp')
- grad_token_gain: float32 [768], replicated
- grad_token_shift: float32 [768], replicated
- grad_small_expand: float32 [196, 384], replicated
- grad_small_expand_bias: float32 [384], replicated
- grad_small_project: float32 [384, 196], replicated
- grad_small_project_bias: float32 [196], replicated
- grad_large_expand: float32 [576, 384], replicated
- grad_large_expand_bias: float32 [384], replicated
- grad_large_project: float32 [384, 576], replicated
- grad_large_project_bias: float32 [576], replicated
- grad_channel_gain: float32 [768], replicated
- grad_channel_shift: float32 [768], replicated
- grad_channel_expand: float32 [768, 3072], P(('dp', 'mp'))
- grad_channel_expand_bias: float32 [3072], replicated
- grad_channel_project: float32 [3072, 768], P(('dp', 'mp'))
- grad_channel_project_bias: float32 [768], replicated
All inputs are finite; a program needn't handle non-finite values.
Results may differ from a plain program's by a relative error of at most 0.008.
Values may be sent and summed in bfloat16 or wider, within the bound.
No kernel may reach another device: no remote copies, remote signals or barrier semaphores. Data moves between devices by JAX's collectives and lax.ppermute only.
A program may use at most 256 MiB of HBM per device.

v0:
```python
import jax
import jax.numpy as jnp
from jax import lax
from jax.sharding import PartitionSpec as P

D = 768


EPS = 1e-06


def gelu_exact(values):
    return jax.nn.gelu(values, approximate=False)


def token_forward(normed, expand, expand_bias, project, project_bias):
    normed_low = normed.astype(jnp.bfloat16)
    before = (
        jnp.einsum("asc,sk->akc", normed_low, expand, preferred_element_type=jnp.float32)
        + expand_bias[None, :, None]
    )
    active = gelu_exact(before).astype(jnp.bfloat16)
    mixed = (
        jnp.einsum("akc,ks->asc", active, project, preferred_element_type=jnp.float32)
        + project_bias[None, :, None]
    )
    return (normed_low, before, active, mixed)


def token_backward(upstream, normed_low, before, active, expand, project):
    grad_project = jnp.einsum("akc,asc->ks", active, upstream, preferred_element_type=jnp.float32)
    grad_project_bias = jnp.sum(upstream.astype(jnp.float32), axis=(0, 2))
    grad_active = jnp.einsum("ks,asc->akc", project, upstream, preferred_element_type=jnp.float32)
    _, pullback = jax.vjp(gelu_exact, before)
    grad_before = pullback(grad_active)[0].astype(jnp.bfloat16)
    grad_expand_bias = jnp.sum(grad_before.astype(jnp.float32), axis=(0, 2))
    grad_expand = jnp.einsum(
        "asc,akc->sk", normed_low, grad_before, preferred_element_type=jnp.float32
    )
    grad_normed = jnp.einsum("sk,akc->asc", expand, grad_before, preferred_element_type=jnp.float32)
    return (grad_expand, grad_expand_bias, grad_project, grad_project_bias, grad_normed)


def contract_rows(left, right):
    return lax.dot_general(
        left, right, (((0,), (0,)), ((), ())), preferred_element_type=jnp.float32
    )


def contract_cols(left, right):
    return lax.dot_general(
        left, right, (((1,), (1,)), ((), ())), preferred_element_type=jnp.float32
    )


def per_device(
    small_images,
    large_images,
    token_gain,
    token_shift,
    small_expand,
    small_expand_bias,
    small_project,
    small_project_bias,
    large_expand,
    large_expand_bias,
    large_project,
    large_project_bias,
    channel_gain,
    channel_shift,
    channel_expand,
    channel_expand_bias,
    channel_project,
    channel_project_bias,
    small_cotangent,
    large_cotangent,
):
    width = D
    part_width = small_images.shape[2]
    small_raw = small_images.astype(jnp.float32)
    large_raw = large_images.astype(jnp.float32)
    totals = lax.psum(
        (
            jnp.sum(small_raw, -1),
            jnp.sum(small_raw * small_raw, -1),
            jnp.sum(large_raw, -1),
            jnp.sum(large_raw * large_raw, -1),
        ),
        "mp",
    )
    small_mean = totals[0] / width
    small_scale = lax.rsqrt(totals[1] / width - small_mean * small_mean + EPS)[..., None]
    small_hat = (small_raw - small_mean[..., None]) * small_scale
    large_mean = totals[2] / width
    large_scale = lax.rsqrt(totals[3] / width - large_mean * large_mean + EPS)[..., None]
    large_hat = (large_raw - large_mean[..., None]) * large_scale
    small_state = token_forward(
        small_hat * token_gain + token_shift,
        small_expand,
        small_expand_bias,
        small_project,
        small_project_bias,
    )
    large_state = token_forward(
        large_hat * token_gain + token_shift,
        large_expand,
        large_expand_bias,
        large_project,
        large_project_bias,
    )
    small_middle = (small_raw + small_state[3]).astype(jnp.bfloat16)
    large_middle = (large_raw + large_state[3]).astype(jnp.bfloat16)
    small_half, large_half = (
        lax.all_to_all(small_middle, "mp", split_axis=1, concat_axis=2, tiled=True),
        lax.all_to_all(large_middle, "mp", split_axis=1, concat_axis=2, tiled=True),
    )
    small_count = small_half.shape[0] * small_half.shape[1]
    rows_raw = jnp.concatenate(
        [small_half.reshape(-1, width), large_half.reshape(-1, width)], 0
    ).astype(jnp.float32)
    row_mean = jnp.mean(rows_raw, -1, keepdims=True)
    row_scale = lax.rsqrt(
        jnp.mean(rows_raw * rows_raw, -1, keepdims=True) - row_mean * row_mean + EPS
    )
    row_hat = (rows_raw - row_mean) * row_scale
    normed_two = (row_hat * channel_gain + channel_shift).astype(jnp.bfloat16)
    hidden_pre = (
        jnp.dot(normed_two, channel_expand, preferred_element_type=jnp.float32)
        + channel_expand_bias
    )
    hidden_act = gelu_exact(hidden_pre).astype(jnp.bfloat16)
    rows_out = (
        rows_raw
        + jnp.dot(hidden_act, channel_project, preferred_element_type=jnp.float32)
        + channel_project_bias
    ).astype(jnp.bfloat16)
    small_output = rows_out[:small_count].reshape(small_half.shape)
    large_output = rows_out[small_count:].reshape(large_half.shape)
    upstream = jnp.concatenate(
        [small_cotangent.reshape(-1, width), large_cotangent.reshape(-1, width)], 0
    )
    upstream_full = upstream.astype(jnp.float32)
    grad_project_bias = jnp.sum(upstream_full, 0)
    grad_hidden = contract_cols(upstream, channel_project)
    _, gelu_pull = jax.vjp(gelu_exact, hidden_pre)
    grad_pre = gelu_pull(grad_hidden)[0].astype(jnp.bfloat16)
    grad_expand_bias = jnp.sum(grad_pre.astype(jnp.float32), 0)
    grad_expand_full = contract_rows(normed_two, grad_pre)
    grad_project_full = contract_rows(hidden_act, upstream)
    grad_expand_part, grad_project_part = (
        lax.psum_scatter(grad_expand_full, ("dp", "mp"), scatter_dimension=0, tiled=True),
        lax.psum_scatter(grad_project_full, ("dp", "mp"), scatter_dimension=0, tiled=True),
    )
    grad_normed_two = contract_cols(grad_pre, channel_expand)
    grad_gain_two = jnp.sum(grad_normed_two * row_hat, 0)
    grad_shift_two = jnp.sum(grad_normed_two, 0)
    scaled_two = grad_normed_two * channel_gain
    grad_rows = upstream_full + row_scale * (
        scaled_two
        - jnp.mean(scaled_two, -1, keepdims=True)
        - row_hat * jnp.mean(scaled_two * row_hat, -1, keepdims=True)
    )
    grad_rows_low = grad_rows.astype(jnp.bfloat16)
    small_back, large_back = (
        lax.all_to_all(
            grad_rows_low[:small_count].reshape(small_half.shape),
            "mp",
            split_axis=2,
            concat_axis=1,
            tiled=True,
        ),
        lax.all_to_all(
            grad_rows_low[small_count:].reshape(large_half.shape),
            "mp",
            split_axis=2,
            concat_axis=1,
            tiled=True,
        ),
    )
    small_grads = token_backward(
        small_back, small_state[0], small_state[1], small_state[2], small_expand, small_project
    )
    large_grads = token_backward(
        large_back, large_state[0], large_state[1], large_state[2], large_expand, large_project
    )
    small_scaled = small_grads[4] * token_gain
    large_scaled = large_grads[4] * token_gain
    back_totals = lax.psum(
        (
            jnp.sum(small_scaled, -1),
            jnp.sum(small_scaled * small_hat, -1),
            jnp.sum(large_scaled, -1),
            jnp.sum(large_scaled * large_hat, -1),
        ),
        "mp",
    )
    small_input_grad = (
        small_back.astype(jnp.float32)
        + small_scale
        * (
            small_scaled
            - back_totals[0][..., None] / width
            - small_hat * (back_totals[1][..., None] / width)
        )
    ).astype(jnp.bfloat16)
    large_input_grad = (
        large_back.astype(jnp.float32)
        + large_scale
        * (
            large_scaled
            - back_totals[2][..., None] / width
            - large_hat * (back_totals[3][..., None] / width)
        )
    ).astype(jnp.bfloat16)
    gain_local = jnp.sum(small_grads[4] * small_hat, axis=(0, 1)) + jnp.sum(
        large_grads[4] * large_hat, axis=(0, 1)
    )
    shift_local = jnp.sum(small_grads[4], axis=(0, 1)) + jnp.sum(large_grads[4], axis=(0, 1))
    offset = lax.axis_index("mp") * part_width
    blank = jnp.zeros((width,), jnp.float32)
    gain_spread = lax.dynamic_update_slice(blank, gain_local, (offset,))
    shift_spread = lax.dynamic_update_slice(blank, shift_local, (offset,))
    summed = lax.psum(
        (
            gain_spread,
            shift_spread,
            small_grads[0],
            small_grads[1],
            small_grads[2],
            small_grads[3],
            large_grads[0],
            large_grads[1],
            large_grads[2],
            large_grads[3],
            grad_gain_two,
            grad_shift_two,
            grad_expand_bias,
            grad_project_bias,
        ),
        ("dp", "mp"),
    )
    return (
        small_output,
        large_output,
        small_input_grad,
        large_input_grad,
        summed[0],
        summed[1],
        summed[2],
        summed[3],
        summed[4],
        summed[5],
        summed[6],
        summed[7],
        summed[8],
        summed[9],
        summed[10],
        summed[11],
        grad_expand_part,
        summed[12],
        grad_project_part,
        summed[13],
    )


def solution(mesh):
    return jax.shard_map(
        per_device,
        mesh=mesh,
        in_specs=(
            P("dp", None, "mp"),
            P("dp", None, "mp"),
            P("mp"),
            P("mp"),
            P(),
            P(),
            P(),
            P(),
            P(),
            P(),
            P(),
            P(),
            P(),
            P(),
            P(),
            P(),
            P(),
            P(),
            P("dp", "mp", None),
            P("dp", "mp", None),
        ),
        out_specs=(
            P("dp", "mp", None),
            P("dp", "mp", None),
            P("dp", None, "mp"),
            P("dp", None, "mp"),
            P(),
            P(),
            P(),
            P(),
            P(),
            P(),
            P(),
            P(),
            P(),
            P(),
            P(),
            P(),
            P(("dp", "mp"), None),
            P(),
            P(("dp", "mp"), None),
            P(),
        ),
        check_vma=False,
    )
```

profile of v0, /device:TPU:0, one launch (start us, length us, event | category | flops | bytes accessed | tf_op | source)
XLA Modules:
  0.0 682.0 jit_solution(10560679393412868089)
XLA Ops:
  7.3 2.3 convert_reduce_fusion.2
  11.0 3.7 all-reduce.3
  19.5 2.0 copy.148
  21.5 6.5 broadcast_subtract_fusion
  29.3 3.3 copy.146
  32.6 2.0 copy.153
  34.6 3.2 copy.154
  39.7 2.4 copy.155
  42.2 4.5 select_select_fusion
  46.7 2.2 copy.157
  48.9 2.7 fusion.42
  53.7 3.7 all-to-all-start
  57.5 8.2 %fusion.41 = (bf16[4,384,384]{2,1,0:T(8,128)(2,1)S(1)}, f32[4,384,384]{2,1,0:T(8,128)}, f32[4,384,384]{1,2,0:T(8,128)}) fusion(f32[384]{0:T(512)S(1)} %copy-done.48, bf16[576,384]{1,0:T(8,128)(2,1)S(1)} %copy-done, bf16[4,576,384]{2,1,0:T(8,128)(2,1)S(1)} %copy-done.18, f32[384]{0:T(512)S(1)} %copy-done.57, f32[384]{0:T(512)S(1)} %copy-done.45, ...), kind=kOutput, calls=%fused_computation.76 | convolution fusion | flops 723714048 | bytes 8133120 | tf_op jit(solution)/shard_map/asc,sk->akc/dot_general | solution.py:19
  66.8 2.6 copy.161
  69.4 3.7 all-to-all-start.1
  73.7 2.0 all-to-all-done.1
  80.7 55.8 %multiply_convert_fusion = (bf16[1544,3072]{1,0:T(8,128)(2,1)}, f32[1544,3072]{1,0:T(8,128)}, f32[1544,3072]{1,0:T(8,128)}) fusion(f32[3072]{0:T(1024)S(1)} %copy-done.52, bf16[768,3072]{1,0:T(8,128)(2,1)} %param.34, f32[768]{0:T(1024)S(1)} %copy-done.54, f32[768]{0:T(1024)S(1)} %copy-done.47, f32[1544]{0:T(1024)S(1)} %get-tuple-element.156, ...), kind=kOutput, calls=%fused_computation.4 | convolution fusion | flops 7609227264 | bytes 54552640 | tf_op jit(solution)/shard_map/dot_general | solution.py:128
  136.5 23.3 %convert_reduce_fusion = (f32[3072]{0:T(1024)S(1)}, bf16[1544,3072]{1,0:T(8,128)(2,1)}) fusion(f32[1544,3072]{1,0:T(8,128)} %get-tuple-element.143, bf16[3072,768]{1,0:T(8,128)(2,1)} %param.36, bf16[1152,768]{1,0:T(8,128)(2,1)S(1)} %bitcast.215, bf16[392,768]{1,0:T(8,128)(2,1)S(1)} %copy-done.25, f32[1544,3072]{1,0:T(8,128)} %get-tuple-element.160, ...), kind=kOutput, calls=%fused_computation.2 | convolution fusion | flops 7370880000 | bytes 54546432 | tf_op jit(solution)/shard_map/dot_general | solution.py:51
  159.8 14.3 %fusion.17 = (f32[768]{0:T(1024)S(1)}, f32[1544]{0:T(1024)S(1)}, f32[1544]{0:T(1024)S(1)}, f32[768]{0:T(1024)S(1)}, f32[1544,768]{1,0:T(8,128)S(1)}) fusion(f32[1544]{0:T(1024)S(1)} %get-tuple-element.156, f32[1544]{0:T(1024)S(1)} %get-tuple-element.155, bf16[1152,768]{1,0:T(8,128)(2,1)S(1)} %bitcast.194, bf16[392,768]{1,0:T(8,128)(2,1)S(1)} %bitcast.207, ...), kind=kOutput, calls=%fused_computation.39 | convolution fusion | flops 7300916224 | bytes 21353600 | tf_op jit(solution)/shard_map/dot_general | solution.py:51
  174.1 3.8 convert_reduce_fusion.3
  182.9 4.3 all-to-all-start.2
  188.6 5.2 copy.173
  193.8 4.9 all-to-all-start.3
  198.7 3.6 copy.194
  203.8 2.5 convolution_bitcast_fusion.3
  206.3 3.9 fusion.44
  210.2 7.1 %copy.195 = bf16[4,288,2,384]{3,2,1,0:T(2,128)(2,1)S(1)} copy(bf16[4,288,2,384]{1,0,3,2:T(4,128)(2,1)} %bitcast.22) | data formatting | bytes 3538944 | tf_op jit(solution)/shard_map/all_to_all | solution.py:172
  219.5 2.0 convolution_bitcast_fusion.1
  222.2 3.8 fusion.39
  226.0 2.0 copy.177
  228.0 3.1 copy.178
  231.1 2.3 convert_reduce_fusion.5
  233.5 2.4 convolution_bitcast_fusion.2
  237.8 3.2 copy.171
  241.0 3.0 convert_reduce_fusion.6
  246.5 14.5 %fusion.99 = f32[768,3072]{1,0:T(8,128)} fusion(bf16[1544,3072]{1,0:T(8,128)(2,1)} %get-tuple-element.167, f32[768]{0:T(1024)S(1)} %copy-done.54, f32[768]{0:T(1024)S(1)} %copy-done.47, f32[1544]{0:T(1024)S(1)} %get-tuple-element.156, f32[1544]{0:T(1024)S(1)} %get-tuple-element.155, bf16[1152,768]{1,0:T(8,128)(2,1)S(1)} %bitcast.196, ...), kind=kOutput, calls=%fused_computation.175 | convolution fusion | flops 7296178176 | bytes 21313600 | tf_op jit(solution)/shard_map/dot_general | solution.py:45
  261.1 14.7 %fusion.98 = f32[3072,768]{1,0:T(8,128)} fusion(bf16[1544,3072]{1,0:T(8,128)(2,1)} %get-tuple-element.142, bf16[1152,768]{1,0:T(8,128)(2,1)} %bitcast.214, bf16[392,768]{1,0:T(8,128)(2,1)} %reshape.120), kind=kOutput, calls=%fused_computation.174 | convolution fusion | flops 7290249216 | bytes 21295104 | tf_op jit(solution)/shard_map/dot_general | solution.py:45
  276.5 12.2 %fusion.20 = bf16[1544,768]{1,0:T(8,128)(2,1)S(1)} fusion(bf16[1544,3072]{1,0:T(8,128)(2,1)} %get-tuple-element.142, bf16[3072,768]{1,0:T(8,128)(2,1)} %param.36, f32[768]{0:T(1024)S(1)} %copy-done.55, bf16[1152,768]{1,0:T(8,128)(2,1)S(1)} %bitcast.197, bf16[392,768]{1,0:T(8,128)(2,1)} %bitcast.210), kind=kOutput, calls=%fused_computation.42 | convolution fusion | flops 7293806592 | bytes 18951168 | tf_op jit(solution)/shard_map/dot_general | solution.py:134
  294.3 3.4 fusion.75
  299.1 4.7 fusion.33
  303.9 3.8 all-reduce.2
  312.0 2.3 reduce_sum.235
  314.5 43.2 %all-reduce = (f32[768]{0:T(1024)}, f32[768]{0:T(1024)}, f32[384]{0:T(512)}, f32[196]{0:T(256)}, f32[384]{0:T(512)}, /*index=5*/f32[576]{0:T(1024)}, f32[768]{0:...) all-reduce(f32[768]{0:T(1024)S(1)} %add_dynamic-update-slice_fusion, ...), channel_id=1, replica_groups=mesh['dp'=16,'mp'=2] {'dp','mp'}, use_global_device_ids=true, to_apply=%region_22.0 | all-reduce | flops 8452 | bytes 67616 | tf_op jit(solution)/shard_map/psum | solution.py:223
  357.7 5.3 fusion.32
  363.0 22.0 %all-reduce.6.cloned.1.call-done = (f32[196,384]{1,0:T(8,128)}, f32[384,196]{0,1:T(8,128)}, f32[576,384]{1,0:T(8,128)}, f32[384,576]{0,1:T(8,128)}) async-done(((f32[196,384]{1,0:T(8,128)}, f32[384,196]{0,1:T(8,128)}, f32[576,384]{1,0:T(8,128)}, f32[384,576]{0,1:T(8,128)}), (f32[196,384]{1,0:T(8,128)}, f32[384,196]{0,1:T(8,128)}, f32[576,384]{1,0:T(8,128)}, ...) | async-done | bytes 2371600 | tf_op jit(solution)/shard_map/psum | solution.py:223
  385.0 141.7 %reduce-scatter.3.cloned.1.call-done = f32[24,3072]{1,0:T(8,128)} async-done(((f32[768,3072]{1,0:T(8,128)}), f32[24,3072]{1,0:T(8,128)}) %reduce-scatter.3.cloned.1.call-update) | async-done | bytes 294928 | tf_op jit(solution)/shard_map/reduce_scatter | solution.py:151
  526.8 142.0 %reduce-scatter.5.cloned.1.call-done = f32[96,768]{1,0:T(8,128)} async-done(((f32[3072,768]{1,0:T(8,128)}), f32[96,768]{1,0:T(8,128)}) %reduce-scatter.5.cloned.1.call-update) | async-done | bytes 294928 | tf_op jit(solution)/shard_map/reduce_scatter | solution.py:152
  672.2 2.1 copy.253
  (184 shorter events, 49.7 us)
Async XLA Ops:
  7.2 50.2 %copy-start = (bf16[576,384]{1,0:T(8,128)(2,1)S(1)}, bf16[576,384]{1,0:T(8,128)(2,1)}, u32[]{:S(2)}) copy-start(bf16[576,384]{1,0:T(8,128)(2,1)} %param.28) | copy-start | bytes 1327108
  7.2 8.2 %copy-start.22 = (bf16[4,196,384]{2,0,1:T(4,128)(2,1)S(1)}, bf16[4,196,384]{2,0,1:T(4,128)(2,1)}, u32[]{:S(2)}) copy-start(bf16[4,196,384]{2,0,1:T(4,128)(2,1)} %param.20) | copy-start | bytes 1806340
  7.2 8.2 %copy-start.45 = (f32[384]{0:T(512)S(1)}, f32[384]{0:T(512)}, u32[]{:S(2)}) copy-start(f32[384]{0:T(512)} %param.22) | copy-start | bytes 4612
  7.2 8.2 %copy-start.57 = (f32[384]{0:T(512)S(1)}, f32[384]{0:T(512)}, u32[]{:S(2)}) copy-start(f32[384]{0:T(512)} %param.23) | copy-start | bytes 4612
  7.2 8.1 %copy-start.50 = (bf16[196,384]{1,0:T(8,128)(2,1)S(1)}, bf16[196,384]{1,0:T(8,128)(2,1)}, u32[]{:S(2)}) copy-start(bf16[196,384]{1,0:T(8,128)(2,1)} %param.24) | copy-start | bytes 451588
  7.3 8.1 %copy-start.56 = (f32[384]{0:T(512)S(1)}, f32[384]{0:T(512)}, u32[]{:S(2)}) copy-start(f32[384]{0:T(512)} %param.25) | copy-start | bytes 4612
  21.5 6.5 copy-start.1
  29.3 3.3 copy-start.17
  34.6 3.2 copy-start.16
  48.9 2.7 copy-start.36
  48.9 2.7 copy-start.59
  51.6 5.8 copy-start.18
  51.6 5.8 copy-start.48
  53.7 15.7 %all-to-all-start = ((bf16[4,196,384]{2,0,1:T(4,128)(2,1)}), bf16[4,196,384]{2,0,1:T(4,128)(2,1)S(1)}, u32[]{:S(2)}, u32[]{:S(2)}) async-start(bf16[4,196,384]{2,0,1:T(4,128)(2,1)} %copy.158), calls=%async_computation | async-start | bytes 1204224 | tf_op jit(solution)/shard_map/all_to_all | solution.py:114
  57.4 8.3 %copy-start.37 = (f32[4,576]{1,0:T(4,128)}, f32[4,576]{1,0:T(4,128)S(1)}, u32[]{:S(2)}) copy-start(f32[4,576]{1,0:T(4,128)S(1)} %get-tuple-element.153) | copy-start | bytes 27652
  57.4 8.3 %copy-start.39 = (f32[4,576]{1,0:T(4,128)}, f32[4,576]{1,0:T(4,128)S(1)}, u32[]{:S(2)}) copy-start(f32[4,576]{1,0:T(4,128)S(1)} %get-tuple-element.154) | copy-start | bytes 27652
  57.5 8.2 %copy-start.34 = (bf16[384,576]{0,1:T(8,128)(2,1)S(1)}, bf16[384,576]{0,1:T(8,128)(2,1)}, u32[]{:S(2)}) copy-start(bf16[384,576]{0,1:T(8,128)(2,1)} %param.30) | copy-start | bytes 1327108
  57.5 8.2 %copy-start.53 = (f32[576]{0:T(1024)S(1)}, f32[576]{0:T(1024)}, u32[]{:S(2)}) copy-start(f32[576]{0:T(1024)} %param.31) | copy-start | bytes 6916
  69.4 6.3 all-to-all-start.1
  73.7 100.4 %copy-start.21 = (bf16[49,8,2,384]{3,1,2,0:T(8,128)(2,1)}, bf16[49,8,2,384]{3,1,2,0:T(8,128)(2,1)S(1)}, u32[]{:S(2)}) copy-start(bf16[49,8,2,384]{3,1,2,0:T(8,128)(2,1)S(1)} %copy.220) | copy-start | bytes 1806340
  78.6 95.5 %copy-start.11 = (bf16[144,8,2,384]{3,1,2,0:T(8,128)(2,1)}, bf16[144,8,2,384]{3,1,2,0:T(8,128)(2,1)S(1)}, u32[]{:S(2)}) copy-start(bf16[144,8,2,384]{3,1,2,0:T(8,128)(2,1)S(1)} %copy.221) | copy-start | bytes 5308420
  80.7 55.8 %copy-start.25 = (bf16[392,768]{1,0:T(8,128)(2,1)S(1)}, bf16[392,768]{1,0:T(8,128)(2,1)}, u32[]{:S(2)}) copy-start(bf16[392,768]{1,0:T(8,128)(2,1)} %reshape.120) | copy-start | bytes 1806340
  80.7 55.8 %copy-start.28 = (bf16[4,288,768]{2,1,0:T(8,128)(2,1)S(1)}, bf16[4,288,768]{2,1,0:T(8,128)(2,1)}, u32[]{:S(2)}) copy-start(bf16[4,288,768]{2,1,0:T(8,128)(2,1)} %param.39) | copy-start | bytes 5308420
  180.2 7.0 %copy-start.14 = (bf16[1544,768]{1,0:T(8,128)(2,1)S(1)}, bf16[1544,768]{1,0:T(8,128)(2,1)}, u32[]{:S(2)}) copy-start(bf16[1544,768]{1,0:T(8,128)(2,1)} %copy-done.13) | copy-start | bytes 7114756
  182.9 10.9 %all-to-all-start.2 = ((bf16[4,98,768]{1,0,2:T(4,128)(2,1)}), bf16[4,98,768]{1,0,2:T(4,128)(2,1)}, u32[]{:S(2)}, u32[]{:S(2)}) async-start(bf16[4,98,768]{1,0,2:T(4,128)(2,1)} %copy.164), calls=%async_computation.2 | async-start | bytes 1572864 | tf_op jit(solution)/shard_map/all_to_all | solution.py:165
  193.8 16.5 %all-to-all-start.3 = ((bf16[4,288,768]{1,0,2:T(4,128)(2,1)}), bf16[4,288,768]{1,0,2:T(4,128)(2,1)}, u32[]{:S(2)}, u32[]{:S(2)}) async-start(bf16[4,288,768]{1,0,2:T(4,128)(2,1)} %copy.173), calls=%async_computation.3 | async-start | bytes 4718592 | tf_op jit(solution)/shard_map/all_to_all | solution.py:172
  198.7 186.4 %all-reduce.6.cloned.1.call-start = ((), (), s32[]{:S(2)}) async-start(), calls=%async_computation.8 | async-start | bytes 4767744 | tf_op jit(solution)/shard_map/psum | solution.py:223
  198.7 7.6 %copy-start.2 = (f32[4,384,384]{2,1,0:T(8,128)S(1)}, f32[4,384,384]{2,1,0:T(8,128)}, u32[]{:S(2)}) copy-start(f32[4,384,384]{2,1,0:T(8,128)} %copy-done.1) | copy-start | bytes 7077892
  202.3 4.0 copy-start.6
  217.3 4.2 copy-start.7
  217.6 3.9 copy-start.9
  219.5 2.7 copy-start.27
  219.5 2.7 copy-start.35
  219.5 2.7 copy-start.49
  231.1 2.3 copy-start.58
  233.4 2.4 copy-start.31
  233.4 2.4 copy-start.15
  237.8 3.2 copy-start.4
  241.0 4.0 copy-start.23
  241.0 4.0 copy-start.42
  241.0 4.0 copy-start.44
  246.4 280.4 %reduce-scatter.3.cloned.1.call-start = ((), (), s32[]{:S(2)}) async-start(), calls=%async_computation.6 | async-start | bytes 9732096 | tf_op jit(solution)/shard_map/reduce_scatter | solution.py:151
  261.1 407.7 %reduce-scatter.5.cloned.1.call-start = ((), (), s32[]{:S(2)}) async-start(), calls=%async_computation.7 | async-start | bytes 9732096 | tf_op jit(solution)/shard_map/reduce_scatter | solution.py:152
  289.5 4.8 copy-start.51
  294.3 4.8 copy-start.20
  303.9 6.9 %copy-start.24 = (bf16[392,768]{1,0:T(8,128)(2,1)S(1)}, bf16[392,768]{1,0:T(8,128)(2,1)}, u32[]{:S(2)}) copy-start(bf16[392,768]{1,0:T(8,128)(2,1)} %slice.16) | copy-start | bytes 1806340
  310.9 46.8 %copy-start.10 = (bf16[4,2,288,384]{3,2,1,0:T(8,128)(2,1)S(1)}, bf16[4,2,288,384]{3,2,1,0:T(8,128)(2,1)}, u32[]{:S(2)}) copy-start(bf16[4,2,288,384]{3,2,1,0:T(8,128)(2,1)} %copy-done.9) | copy-start | bytes 5308420
  385.0 289.3 %copy-start.32 = (f32[384,576]{0,1:T(8,128)S(1)}, f32[384,576]{0,1:T(8,128)}, u32[]{:S(2)}) copy-start(f32[384,576]{0,1:T(8,128)} %get-tuple-element.182) | copy-start | bytes 2654212
  (21 other events, 34.4 us)
Sparse Core Ops, SparseCore 0:
  246.5 138.5 all-reduce.5
  391.5 135.2 reduce-scatter.2
  534.3 134.4 reduce-scatter.4
where the time goes:
time: 691 us; the launch traced here: 682 us
  waiting for transfers between devices  308 us (45%)
  matrix products  170 us (25%)
  local copies, waits for them, and re-layouts  77.8 us (11%)
  blocking collectives  50.7 us (7%)
  other arithmetic  44.5 us (6%)
  starting transfers between devices  16.8 us (2%)
  between operations  14.7 us (2%)
    reduce_scatter x1, waiting for transfers between devices, per_device(): lax.psum_scatter(grad_project_full, ('dp', 'mp'), scatter_dimension=0, ti...  142 us
    reduce_scatter x1, waiting for transfers between devices, per_device(): lax.psum_scatter(grad_expand_full, ('dp', 'mp'), scatter_dimension=0, til...  142 us
    dot_general x1, matrix products, per_device(): jnp.dot(normed_two, channel_expand, preferred_element_type=jnp.float32)  55.8 us
    psum x1, blocking collectives, per_device(): lax.psum((gain_spread, shift_spread, small_grads[0], small_grads[1], smal...  43.2 us
    dot_general x2, matrix products, contract_cols(): lax.dot_general(left, right, (((1,), (1,)), ((), ())), preferred_element_...  37.6 us
    dot_general x2, matrix products, contract_rows(): lax.dot_general(left, right, (((0,), (0,)), ((), ())), preferred_element_...  29.2 us
    psum x1, waiting for transfers between devices, per_device(): lax.psum((gain_spread, shift_spread, small_grads[0], small_grads[1], smal...  22 us
    unnamed x133, local copies, waits for them, and re-layouts  18.3 us
  transfers between devices with their start and end apart: 7, of which 4 were waited for; matrix products, arithmetic and copies ran while one was open for 15% of the time, Pallas kernels for 0%

commit v1 on v0

v1 whole, which is shorter than its diff:
```python
import functools

import jax
import jax.numpy as jnp
from jax import lax
from jax.experimental import pallas as pl
from jax.experimental.pallas import tpu as pltpu
from jax.sharding import PartitionSpec as P

BF = jnp.bfloat16
F32 = jnp.float32
EPS = 1e-06
SQRT_HALF = 0.7071067811865476
INV_SQRT_2PI = 0.3989422804014327
HALF_LOG2E = 0.7213475204444817
NN = ((1,), (0,))
NT = ((1,), (1,))
TN = ((0,), (0,))
MB = 1 << 20
PLANES = 4
ORDER = (0, 3, 1, 2)
VEC = 16


def dot(left, right, dims):
    return lax.dot_general(left, right, (dims, ((), ())), preferred_element_type=F32)


def gelu_pair(values):
    cdf = 0.5 * lax.erf(values * SQRT_HALF) + 0.5
    pdf = jnp.exp2((values * values) * (-HALF_LOG2E)) * INV_SQRT_2PI
    return values * cdf, cdf + values * pdf


def norm(values):
    width = values.shape[-1]
    mean = jnp.sum(values, -1, keepdims=True) * (1.0 / width)
    square = jnp.sum(values * values, -1, keepdims=True) * (1.0 / width)
    scale = lax.rsqrt(square - mean * mean + EPS)
    return (values - mean) * scale, scale


def round_up(value, to):
    return (value + to - 1) // to * to


def params(limit, **extra):
    return pltpu.CompilerParams(vmem_limit_bytes=limit * MB, **extra)


def whole(shape):
    return pl.BlockSpec(shape, lambda *_: (0,) * len(shape))


def load_images(sc, own, other, dest):
    rows, part = own.shape[1], own.shape[2]
    mine = pl.multiple_of(sc[0] * part, 128)
    theirs = pl.multiple_of((1 - sc[0]) * part, 128)
    if dest.shape[0] != rows:
        dest[...] = jnp.zeros_like(dest)
    dest[0:rows, pl.ds(mine, part)] = own[0].astype(F32)
    dest[0:rows, pl.ds(theirs, part)] = other[0].astype(F32)


def load_token_params(sc, own, other, dest):
    part = own.shape[1]
    dest[:, pl.ds(pl.multiple_of(sc[0] * part, 128), part)] = own[...]
    dest[:, pl.ds(pl.multiple_of((1 - sc[0]) * part, 128), part)] = other[...]


def front_kernel(
    sc, xs, xs_in, xl, xl_in, ys, ys_in, yl, yl_in, tok, tok_in,
    es, bes, pjs, bps, el, bel, pjl, bpl, gain2, shift2,
    x1s, n2s, as_, ds_, yrs, x1l, n2l, al, dl, yrl, gy,
    x_s, x_l, tk, y_s,
):
    load_images(sc, xs, xs_in, x_s)
    load_images(sc, xl, xl_in, x_l)
    load_token_params(sc, tok, tok_in, tk)
    first = sc[0] == 0
    half = ys.shape[1]
    mine, theirs = ys[0].astype(F32), ys_in[0].astype(F32)
    y_s[...] = jnp.zeros_like(y_s)
    y_s[0:half, :] = jnp.where(first, mine, theirs)
    y_s[half : 2 * half, :] = jnp.where(first, theirs, mine)
    yrs[0] = y_s[...].astype(BF)
    half = yl.shape[1]
    yrl[0, pl.ds(pl.multiple_of(sc[0] * half, 16), half), :] = yl[0]
    yrl[0, pl.ds(pl.multiple_of((1 - sc[0]) * half, 16), half), :] = yl_in[0]
    sums = jnp.sum(mine, 0, keepdims=True) + jnp.sum(theirs, 0, keepdims=True)
    sums = sums + jnp.sum(yl[0].astype(F32), 0, keepdims=True)
    sums = sums + jnp.sum(yl_in[0].astype(F32), 0, keepdims=True)

    @pl.when(pl.program_id(0) == 0)
    def _():
        gy[...] = sums

    @pl.when(pl.program_id(0) != 0)
    def _():
        gy[...] += sums

    gain, shift = tk[0:1, :], tk[1:2, :]

    def group(x_ref, e, be, pj, bp, x1, n2, a_ref, d_ref):
        x = x_ref[...]
        hat, _ = norm(x)
        normed = (hat * gain + shift).astype(BF)
        active, slope = gelu_pair(dot(e[...], normed, TN) + be[...])
        active = active.astype(BF)
        a_ref[0] = active
        d_ref[0] = slope
        middle = (x_ref[...] + (dot(pj[...], active, TN) + bp[...])).astype(BF)
        x1[0] = middle
        hat2, _ = norm(middle.astype(F32))
        n2[0] = (hat2 * gain2[...] + shift2[...]).astype(BF)

    group(x_s, es, bes, pjs, bps, x1s, n2s, as_, ds_)
    group(x_l, el, bel, pjl, bpl, x1l, n2l, al, dl)


def own_image(rows, width, count):
    return pl.BlockSpec((1, rows, width), lambda i, sc: (sc[0] * count + i, 0, 0))


def per_image(rows, width):
    return pl.BlockSpec((1, rows, width), lambda i, sc: (i, 0, 0))


def front(sc, xs, xs_in, xl, xl_in, ys, ys_in, yl, yl_in, tok, tok_in, token_s, token_l, gain2, shift2):
    count, small, part = xs_in.shape
    large = xl_in.shape[1]
    width = 2 * part
    hidden = token_s[0].shape[1]
    pad_s = token_s[0].shape[0]
    pad_l = token_l[0].shape[0]
    hs, hl = ys.shape[1], yl.shape[1]
    outs = []
    for rows in (pad_s, pad_l):
        outs += [
            ((count, rows, width), BF),
            ((count, rows, width), BF),
            ((count, hidden, width), BF),
            ((count, hidden, width), F32),
            ((count, rows, width), BF),
        ]
    return pl.pallas_call(
        front_kernel,
        grid_spec=pltpu.PrefetchScalarGridSpec(
            num_scalar_prefetch=1,
            grid=(count,),
            in_specs=[
                own_image(small, part, count), per_image(small, part),
                own_image(large, part, count), per_image(large, part),
                own_image(hs, width, count), per_image(hs, width),
                own_image(hl, width, count), per_image(hl, width),
                whole(tok.shape), whole(tok.shape),
            ]
            + [whole(w.shape) for w in token_s + token_l]
            + [whole((1, width))] * 2,
            out_specs=[per_image(*shape[1:]) for shape, _ in outs] + [whole((1, width))],
            scratch_shapes=[
                pltpu.VMEM((pad_s, width), F32),
                pltpu.VMEM((pad_l, width), F32),
                pltpu.VMEM((2, width), F32),
                pltpu.VMEM((pad_s, width), F32),
            ],
        ),
        out_shape=[jax.ShapeDtypeStruct(*o) for o in outs] + [jax.ShapeDtypeStruct((1, width), F32)],
        compiler_params=params(56),
        name="front",
    )(sc, xs, xs_in, xl, xl_in, ys, ys_in, yl, yl_in, tok, tok_in, *token_s, *token_l, gain2, shift2)


def channel_kernel(is_first, is_last, *refs):
    refs = list(refs)
    sc = refs.pop(0)
    n2s, n2l, ys, yl, w1, b1, w2 = [refs.pop(0) for _ in range(7)]
    if not is_first:
        out_in, dn_in = refs.pop(0), refs.pop(0)
    if is_last:
        x1s, x1l, gain2, b2 = [refs.pop(0) for _ in range(4)]
    send, keep, gb1 = [refs.pop(0) for _ in range(3)]
    if is_last:
        out_rows, dx1, g2 = [refs.pop(0) for _ in range(3)]
    else:
        out_acc, dn_acc = refs.pop(0), refs.pop(0)
    n2, y, acts, grads, out, dn, sems = refs
    rows, width = n2.shape
    small = n2s.shape[0]
    hidden = w1.shape[1]
    if not is_first:
        loads = [
            pltpu.make_async_copy(out_in, out, sems.at[0]),
            pltpu.make_async_copy(dn_in, dn, sems.at[1]),
        ]
        for copy in loads:
            copy.start()
    n2[0:small, :] = n2s[...]
    n2[small:rows, :] = n2l[...]
    y[0:small, :] = ys[...]
    y[small:rows, :] = yl[...]
    tile = rows // 2
    bias_grad = jnp.zeros((1, hidden), F32)
    for step in range(2):
        at = pl.ds(step * tile, tile)
        active, slope = gelu_pair(dot(n2[at, :], w1[...], NN) + b1[...])
        grad = dot(y[at, :], w2[...], NT) * slope
        bias_grad = bias_grad + jnp.sum(grad, 0, keepdims=True)
        acts[at, :] = active.astype(BF)
        grads[at, :] = grad.astype(BF)
    gb1[...] = bias_grad
    if not is_first:
        for copy in loads:
            copy.wait()
    for step in range(2):
        at = pl.ds(step * tile, tile)
        mixed = dot(acts[at, :], w2[...], NN)
        back = dot(grads[at, :], w1[...], NT)
        if is_first:
            out[at, :] = mixed
            dn[at, :] = back
        else:
            out[at, :] += mixed
            dn[at, :] += back
    if is_last:
        gain_sum = jnp.zeros((1, width), F32)
        shift_sum = jnp.zeros((1, width), F32)
        for low, high, ref in ((0, small, x1s), (small, rows, x1l)):
            middle = ref[...].astype(F32)
            out_rows[low:high, :] = (middle + out[low:high, :] + b2[...]).astype(BF)
            hat, scale = norm(middle)
            back = dn[low:high, :]
            gain_sum = gain_sum + jnp.sum(back * hat, 0, keepdims=True)
            shift_sum = shift_sum + jnp.sum(back, 0, keepdims=True)
            scaled = back * gain2[...]
            mean = jnp.sum(scaled, -1, keepdims=True) * (1.0 / width)
            along = jnp.sum(scaled * hat, -1, keepdims=True) * (1.0 / width)
            dx1[low:high, :] = (
                y[low:high, :].astype(F32) + scale * (scaled - mean - hat * along)
            ).astype(BF)
        g2[0:1, :] = gain_sum
        g2[1:2, :] = shift_sum
    else:
        stores = [
            pltpu.make_async_copy(out, out_acc, sems.at[0]),
            pltpu.make_async_copy(dn, dn_acc, sems.at[1]),
        ]
        for copy in stores:
            copy.start()
    first = sc[0] == 0
    quarter = width // 32
    expand = dot(n2[...], grads[...], TN).reshape(PLANES, 4, 2, quarter, hidden)
    for c in range(4):
        low = expand[:, c, 0].reshape(PLANES * quarter, hidden)
        high = expand[:, c, 1].reshape(PLANES * quarter, hidden)
        keep[c, 0 : PLANES * quarter, :] = jnp.where(first, low, high).astype(BF)
        send[c, 0 : PLANES * quarter, :] = jnp.where(first, high, low).astype(BF)
    project = dot(acts[...], y[...], TN).reshape(4, 2, hidden // 8, width)
    for c in range(4):
        low, high = project[c, 0], project[c, 1]
        keep[c, PLANES * quarter :, :] = jnp.where(first, low, high).astype(BF)
        send[c, PLANES * quarter :, :] = jnp.where(first, high, low).astype(BF)
    if not is_last:
        for copy in stores:
            copy.wait()


def channel(sc, plane, is_first, is_last, rows_in, w1, b1, w2, carried, ending):
    n2s, n2l, ys, yl = rows_in
    small, width = n2s.shape
    rows = small + n2l.shape[0]
    hidden = w1.shape[1] // PLANES
    any_spec = pl.BlockSpec(memory_space=pl.ANY)
    in_specs = [whole(a.shape) for a in rows_in] + [
        pl.BlockSpec((width, hidden), lambda i, sc: (0, plane)),
        pl.BlockSpec((1, hidden), lambda i, sc: (0, plane)),
        pl.BlockSpec((hidden, width), lambda i, sc: (plane, 0)),
    ]
    in_specs += [any_spec for _ in carried] + [whole(a.shape) for a in ending]
    block = (4, width // 8 + hidden // 8, width)
    outs = [(block, BF), (block, BF), ((1, hidden), F32)]
    out_specs = [whole(s) for s, _ in outs]
    if is_last:
        extra = [((rows, width), BF), ((rows, width), BF), ((2, width), F32)]
        out_specs += [whole(s) for s, _ in extra]
    else:
        extra = [((rows, width), F32)] * 2
        out_specs += [any_spec] * 2
    flops = 6 * 2 * rows * width * hidden
    return pl.pallas_call(
        functools.partial(channel_kernel, is_first, is_last),
        grid_spec=pltpu.PrefetchScalarGridSpec(
            num_scalar_prefetch=1,
            grid=(1,),
            in_specs=in_specs,
            out_specs=out_specs,
            scratch_shapes=[
                pltpu.VMEM((rows, width), BF),
                pltpu.VMEM((rows, width), BF),
                pltpu.VMEM((rows, hidden), BF),
                pltpu.VMEM((rows, hidden), BF),
                pltpu.VMEM((rows, width), F32),
                pltpu.VMEM((rows, width), F32),
                pltpu.SemaphoreType.DMA((2,)),
            ],
        ),
        out_shape=[jax.ShapeDtypeStruct(*o) for o in outs + extra],
        compiler_params=params(60),
        cost_estimate=pl.CostEstimate(flops=flops, bytes_accessed=20 * MB, transcendentals=2 * rows * hidden),
        name="channel",
    )(sc, *rows_in, w1, b1, w2, *carried, *ending)


def back_kernel(
    sc, dxs, dxl, xs, xs_in, xl, xl_in, tok, tok_in,
    as_, ds_, al, dl, es, pjs, el, pjl, g2, gy, b1a, b1b, b1c, b1d,
    gis_keep, gis_send, gil_keep, gil_send, w_keep, w_send, vec,
    x_s, x_l, tk, gps, ges, gpl, gel, gi_s, gi_l,
):
    step = pl.program_id(0)
    load_images(sc, xs, xs_in, x_s)
    load_images(sc, xl, xl_in, x_l)
    load_token_params(sc, tok, tok_in, tk)
    gain, shift = tk[0:1, :], tk[1:2, :]

    @pl.when(step == 0)
    def _():
        vec[...] = jnp.zeros_like(vec)
        for ref in (gps, ges, gpl, gel):
            ref[...] = jnp.zeros_like(ref)

    def group(x_ref, dx, a, d, e, pj, gp, ge, be_at, bp_row, gi, keep, send):
        rows, width = x_ref.shape
        hidden = a.shape[1]
        dx = dx[0]
        hat, scale = norm(x_ref[...])
        normed = (hat * gain + shift).astype(BF)
        gp[0:rows, :] += dot(dx, a[0], NT)
        before = (dot(pj[...], dx, NN) * d[0]).astype(BF)
        ge[0:rows, :] += dot(normed, before, NT)
        ones = jnp.ones((8, width), BF)
        vec[bp_row : bp_row + 1, 0:rows] += dot(ones, dx, NT)[0:1, :]
        vec[9:10, be_at : be_at + hidden] += dot(ones, before, NT)[0:1, :]
        grad = dot(e[...], before, NN)
        vec[0:1, :] += jnp.sum(grad * hat, 0, keepdims=True)
        vec[1:2, :] += jnp.sum(grad, 0, keepdims=True)
        scaled = grad * gain
        mean = jnp.sum(scaled, -1, keepdims=True) * (1.0 / width)
        along = jnp.sum(scaled * hat, -1, keepdims=True) * (1.0 / width)
        gi[...] = dx.astype(F32) + scale * (scaled - mean - hat * along)
        part = width // 2
        count = keep.shape[1]
        keep[0] = gi[0:count, pl.ds(pl.multiple_of(sc[0] * part, 128), part)].astype(BF)
        send[0] = gi[0:count, pl.ds(pl.multiple_of((1 - sc[0]) * part, 128), part)].astype(BF)

    hidden = as_.shape[1]
    group(x_s, dxs, as_, ds_, es, pjs, gps, ges, 0, 10, gi_s, gis_keep, gis_send)
    group(x_l, dxl, al, dl, el, pjl, gpl, gel, hidden, 11, gi_l, gil_keep, gil_send)

    @pl.when(step == pl.num_programs(0) - 1)
    def _():
        vec[2:4, :] = g2[...]
        vec[4:5, :] = gy[...]
        for i, ref in enumerate((b1a, b1b, b1c, b1d)):
            vec[5 + i : 6 + i, :] = ref[...]
        size = w_keep.shape[2]
        half_s, half_l = gps.shape[0] // 2, gpl.shape[0] // 2
        for side, ref in ((sc[0], w_keep), (1 - sc[0], w_send)):
            for t, (small, large) in enumerate(((gps, gpl), (ges, gel))):
                at = pl.multiple_of(side * half_s, 8)
                ref[0, t] = small[pl.ds(at, size), :].astype(BF)
                for c in range(1, 4):
                    have = min(size, half_l - (c - 1) * size)
                    at = pl.multiple_of(side * half_l + (c - 1) * size, 8)
                    ref[c, t, 0:have, :] = large[pl.ds(at, have), :].astype(BF)
                    if have < size:
                        ref[c, t, have:, :] = jnp.zeros((size - have, hidden), BF)


def back(sc, dxs, dxl, xs, xs_in, xl, xl_in, tok, tok_in, saved, weights, vectors):
    count, small, part = xs_in.shape
    large = xl_in.shape[1]
    width = 2 * part
    pad_s, pad_l = dxs.shape[1], dxl.shape[1]
    hidden = saved[0].shape[1]
    size = piece_rows(pad_s, pad_l)
    outs = [
        ((count, small, part), BF),
        ((count, small, part), BF),
        ((count, large, part), BF),
        ((count, large, part), BF),
        ((4, 2, size, hidden), BF),
        ((4, 2, size, hidden), BF),
        ((VEC, width), F32),
    ]
    return pl.pallas_call(
        back_kernel,
        grid_spec=pltpu.PrefetchScalarGridSpec(
            num_scalar_prefetch=1,
            grid=(count,),
            in_specs=[
                per_image(pad_s, width), per_image(pad_l, width),
                own_image(small, part, count), per_image(small, part),
                own_image(large, part, count), per_image(large, part),
                whole(tok.shape), whole(tok.shape),
            ]
            + [per_image(hidden, width)] * 4
            + [whole(a.shape) for a in weights]
            + [whole(a.shape) for a in vectors],
            out_specs=[per_image(*s[1:]) for s, _ in outs[:4]] + [whole(s) for s, _ in outs[4:]],
            scratch_shapes=[
                pltpu.VMEM((pad_s, width), F32),
                pltpu.VMEM((pad_l, width), F32),
                pltpu.VMEM((2, width), F32),
                pltpu.VMEM((2 * size, hidden), F32),
                pltpu.VMEM((2 * size, hidden), F32),
                pltpu.VMEM((pad_l, hidden), F32),
                pltpu.VMEM((pad_l, hidden), F32),
                pltpu.VMEM((pad_s, width), F32),
                pltpu.VMEM((pad_l, width), F32),
            ],
        ),
        out_shape=[jax.ShapeDtypeStruct(*o) for o in outs],
        compiler_params=params(56),
        name="back",
    )(sc, dxs, dxl, xs, xs_in, xl, xl_in, tok, tok_in, *saved, *weights, *vectors)


def piece_rows(pad_s, pad_l):
    return max(round_up(pad_s // 2, 16), round_up(-(-(pad_l // 2) // 3), 16))


def total4(parts):
    a, b, c, d = [p.astype(F32) for p in parts]
    return (a + b) + (c + d)


def pair_kernel(count, sc, *refs):
    keeps, recvs, outs = refs[:4], refs[4:8], refs[8:12]
    for a, b, o in zip(keeps, recvs, outs):
        o[...] = (a[0].astype(F32) + b[0].astype(F32)).astype(BF)
    for k in range(count):
        refs[12 + k][...] = refs[12 + count + k][...]


def pair_sum(sc, keep, recv):
    block = keep.shape[1:]
    zeros = (0,) * len(block)
    specs = [
        pl.BlockSpec((1,) + block, lambda i, sc, k=k: (sc[1] ^ k,) + zeros) for k in range(4)
    ]
    return pl.pallas_call(
        functools.partial(pair_kernel, 0),
        grid_spec=pltpu.PrefetchScalarGridSpec(
            num_scalar_prefetch=1,
            grid=(1,),
            in_specs=specs * 2,
            out_specs=[whole(block)] * 4,
        ),
        out_shape=[jax.ShapeDtypeStruct(block, BF)] * 4,
        compiler_params=params(32),
        name="pair_sum",
    )(sc, *([keep] * 4), *([recv] * 4))


def quad_kernel(sc, own, r1, r2, r3, d0, d1, d2, d3, rest, hold):
    rows = own.shape[0] // 2
    hold[...] = total4([r[0:rows, :] for r in (own, r1, r2, r3)]).reshape(hold.shape)
    rest[...] = total4([r[rows:, :] for r in (own, r1, r2, r3)]).astype(BF)
    for k, ref in enumerate((d0, d1, d2, d3)):
        ref[...] = hold[sc[2] ^ k].astype(BF)


def quad_sum(sc, own, received):
    rows, width = own.shape
    piece = (rows // 2 // PLANES, width)
    return pl.pallas_call(
        quad_kernel,
        grid_spec=pltpu.PrefetchScalarGridSpec(
            num_scalar_prefetch=1,
            grid=(1,),
            in_specs=[whole(own.shape)] * 4,
            out_specs=[whole(piece)] * 4 + [whole((rows // 2, width))],
            scratch_shapes=[pltpu.VMEM((PLANES,) + piece, F32)],
        ),
        out_shape=[jax.ShapeDtypeStruct(piece, BF)] * 4 + [jax.ShapeDtypeStruct((rows // 2, width), BF)],
        compiler_params=params(32),
        name="quad_sum",
    )(sc, own, *received)


def last_kernel(sc, *refs):
    expand_out, project_out = refs[-2:]
    width = refs[0].shape[1]
    for plane in range(PLANES):
        expand_out[:, plane * width : (plane + 1) * width] = total4(
            [r[...] for r in refs[4 * plane : 4 * plane + 4]]
        )
        parts = refs[16 + 4 * plane : 20 + 4 * plane]

        @pl.when(sc[2] == plane)
        def _():
            project_out[...] = total4([r[...] for r in parts])


def last_sum(sc, expands, projects):
    flat = [a for plane in range(PLANES) for a in expands[plane]]
    flat += [a for plane in range(PLANES) for a in projects[plane]]
    rows, width = flat[0].shape
    outs = [(rows, PLANES * width), flat[-1].shape]
    return pl.pallas_call(
        last_kernel,
        grid_spec=pltpu.PrefetchScalarGridSpec(
            num_scalar_prefetch=1,
            grid=(1,),
            in_specs=[whole(a.shape) for a in flat],
            out_specs=[whole(s) for s in outs],
        ),
        out_shape=[jax.ShapeDtypeStruct(s, F32) for s in outs],
        compiler_params=params(32),
        name="last_sum",
    )(sc, *flat)


def token_sum_kernel(*refs):
    w, v = refs[-2:]
    w[...] = total4([r[...] for r in refs[0:4]]).astype(BF)
    v[...] = total4([r[...] for r in refs[4:8]])


def token_sum(ws, vs):
    return pl.pallas_call(
        token_sum_kernel,
        out_shape=[jax.ShapeDtypeStruct(ws[0].shape, BF), jax.ShapeDtypeStruct(vs[0].shape, F32)],
        compiler_params=params(32),
        name="token_sum",
    )(*ws, *vs)


def unpack_kernel(sc, *refs):
    mine, theirs = refs[0:4], refs[4:8]
    vec = refs[8]
    ges, gps, gel, gpl = refs[9:13]
    vectors = refs[13:23]
    hold, flip_s, flip_l = refs[23:]
    for k in range(4):
        hold[sc[0], sc[1] ^ k] = mine[k][...]
        hold[1 - sc[0], sc[1] ^ k] = theirs[k][...]
    size = mine[0].shape[1]
    small, large = ges.shape[0], gel.shape[0]
    for side in range(2):
        low = side * size
        have = min(size, small - low)
        ges[low : low + have, :] = hold[side, 0, 1].astype(F32)[0:have, :]
        flip_s[low : low + size, :] = hold[side, 0, 0].astype(F32)
        for c in range(1, 4):
            low = side * (large // 2) + (c - 1) * size
            have = min(size, large // 2 - (c - 1) * size)
            gel[low : low + have, :] = hold[side, c, 1].astype(F32)[0:have, :]
            flip_l[low : low + have, :] = hold[side, c, 0].astype(F32)[0:have, :]
    gps[...] = flip_s[...].T[:, 0:small]
    gpl[...] = flip_l[...].T[:, 0:large]
    hidden = ges.shape[1]
    picks = [(0, 0), (1, 0), (9, 0), (10, 0), (9, hidden), (11, 0), (2, 0), (3, 0), None, (4, 0)]
    for ref, pick in zip(vectors, picks):
        if pick is None:
            width = vec.shape[1]
            for i in range(ref.shape[1] // width):
                ref[0:1, i * width : (i + 1) * width] = vec[5 + i : 6 + i, :]
        else:
            row, at = pick
            ref[...] = vec[row : row + 1, at : at + ref.shape[1]]


def unpack(sc, mine, theirs, vec, small, large, hidden, channel_hidden):
    width = vec.shape[1]
    size = mine[0].shape[1]
    outs = [(small, hidden), (hidden, small), (large, hidden), (hidden, large)]
    outs += [(1, n) for n in (width, width, hidden, small, hidden, large, width, width, channel_hidden, width)]
    return pl.pallas_call(
        unpack_kernel,
        grid_spec=pltpu.PrefetchScalarGridSpec(
            num_scalar_prefetch=1,
            grid=(1,),
            in_specs=[whole(a.shape) for a in mine + theirs] + [whole(vec.shape)],
            out_specs=[whole(s) for s in outs],
            scratch_shapes=[
                pltpu.VMEM((2, 4) + mine[0].shape, BF),
                pltpu.VMEM((round_up(2 * size, 128), hidden), F32),
                pltpu.VMEM((round_up(large, 128), hidden), F32),
            ],
        ),
        out_shape=[jax.ShapeDtypeStruct(s, F32) for s in outs],
        compiler_params=params(32),
        name="unpack",
    )(sc, *mine, *theirs, vec)


def swap(values):
    return lax.ppermute(values, "mp", [(0, 1), (1, 0)])


def across(values, mask, pairs):
    return lax.ppermute(values, "dp", [(i, i ^ mask) for i in pairs])


def per_device(
    chips,
    small_images,
    large_images,
    token_gain,
    token_shift,
    small_expand,
    small_expand_bias,
    small_project,
    small_project_bias,
    large_expand,
    large_expand_bias,
    large_project,
    large_project_bias,
    channel_gain,
    channel_shift,
    channel_expand,
    channel_expand_bias,
    channel_project,
    channel_project_bias,
    small_cotangent,
    large_cotangent,
):
    core = lax.axis_index("mp")
    chip = lax.axis_index("dp")
    sc = jnp.stack([core, chip % 4, (chip // 4) % PLANES]).astype(jnp.int32)
    count = small_images.shape[0] // 2
    small, large = small_images.shape[1], large_images.shape[1]
    width = channel_expand.shape[0]
    hidden = small_expand.shape[1]
    pad_s, pad_l = round_up(small, 16), round_up(large, 16)

    def theirs(values):
        return lax.dynamic_slice_in_dim(values, (1 - core) * count, count, 0)

    xs_in, xl_in = swap(theirs(small_images)), swap(theirs(large_images))
    tok = jnp.stack([token_gain, token_shift])
    tok_in = swap(tok)
    ys_in, yl_in = swap(theirs(small_cotangent)), swap(theirs(large_cotangent))

    def token_weights(expand, expand_bias, project, project_bias, pad):
        extra = pad - expand.shape[0]
        return [
            jnp.pad(expand, ((0, extra), (0, 0))),
            expand_bias[:, None],
            jnp.pad(project, ((0, 0), (0, extra))),
            jnp.pad(project_bias, (0, extra))[:, None],
        ]

    token_s = token_weights(small_expand, small_expand_bias, small_project, small_project_bias, pad_s)
    token_l = token_weights(large_expand, large_expand_bias, large_project, large_project_bias, pad_l)
    gain2, shift2 = channel_gain[None], channel_shift[None]
    (x1s, n2s, as_, ds_, yrs, x1l, n2l, al, dl, yrl, gy) = front(
        sc, small_images, xs_in, large_images, xl_in, small_cotangent, ys_in, large_cotangent, yl_in,
        tok, tok_in, token_s, token_l, gain2, shift2,
    )

    def rows(values):
        return values.reshape(-1, width)

    rows_in = [rows(n2s), rows(n2l), rows(yrs), rows(yrl)]
    carried = []
    sends, keeps, b1_grads = {}, {}, {}
    for i, plane in enumerate(ORDER):
        is_first, is_last = i == 0, i == PLANES - 1
        ending = [rows(x1s), rows(x1l), gain2, channel_project_bias[None]] if is_last else []
        sends[plane], keeps[plane], b1_grads[plane], *carried = channel(
            sc, plane, is_first, is_last, rows_in,
            channel_expand, channel_expand_bias[None], channel_project, carried, ending,
        )
    out_rows, dx1, g2 = carried
    cut = count * pad_s
    dxs = dx1[:cut].reshape(count, pad_s, width)
    dxl = dx1[cut:].reshape(count, pad_l, width)
    gis_keep, gis_send, gil_keep, gil_send, w_keep, w_send, vec = back(
        sc, dxs, dxl, small_images, xs_in, large_images, xl_in, tok, tok_in,
        [as_, ds_, al, dl],
        [token_s[0], token_s[2], token_l[0], token_l[2]],
        [g2, gy] + [b1_grads[plane] for plane in range(PLANES)],
    )

    def whole_images(keep, received):
        keep_first = jnp.concatenate([keep, received], 0)
        keep_last = jnp.concatenate([received, keep], 0)
        return jnp.where(core == 0, keep_first, keep_last)

    def halves(values):
        half = values.shape[1] // 2
        parts = values.reshape(count, 2, half, width)
        mine = lax.dynamic_index_in_dim(parts, core, 1, False)
        other = lax.dynamic_index_in_dim(parts, 1 - core, 1, False)
        return whole_images(mine, swap(other))

    small_output = halves(out_rows[:cut].reshape(count, pad_s, width)[:, :small])
    large_output = halves(out_rows[cut:].reshape(count, pad_l, width)[:, :large])
    small_input_grad = whole_images(gis_keep, swap(gis_send))
    large_input_grad = whole_images(gil_keep, swap(gil_send))

    if chips == 4 * PLANES:
        everyone = range(chips)
        expands, projects = {}, {}
        for plane in ORDER:
            own, *others = pair_sum(sc, keeps[plane], swap(sends[plane]))
            received = [across(o, k + 1, everyone) for k, o in enumerate(others)]
            d0, d1, d2, d3, rest = quad_sum(sc, own, received)
            expands[plane] = [d0] + [across(d, 4 * k, everyone) for k, d in ((1, d1), (2, d2), (3, d3))]
            projects[plane] = [rest] + [
                across(rest, 4 * k, [4 * (plane ^ k) + c for c in range(4)]) for k in (1, 2, 3)
            ]
        expand_part, project_part = last_sum(sc, expands, projects)
        own, *others = pair_sum(sc, w_keep, swap(w_send))
        vec = vec + swap(vec)
        w, v = token_sum(
            [own] + [across(o, k + 1, everyone) for k, o in enumerate(others)],
            [vec] + [across(vec, k, everyone) for k in (1, 2, 3)],
        )
        w, v = token_sum(
            [w] + [across(w, 4 * k, everyone) for k in (1, 2, 3)],
            [v] + [across(v, 4 * k, everyone) for k in (1, 2, 3)],
        )
        mine = [w] + [across(w, k, everyone) for k in (1, 2, 3)]
    else:
        def both(keep, send):
            return jnp.where(core == 0, jnp.stack([keep, send]), jnp.stack([send, keep])).astype(F32)

        expand_full, project_full = [], []
        for plane in range(PLANES):
            parts = both(keeps[plane], sends[plane])
            cut_rows = width // 8
            e = parts[:, :, :cut_rows].reshape(2, 4, PLANES, width // 32, -1)
            expand_full.append(e.transpose(2, 1, 0, 3, 4).reshape(width, -1))
            project_full.append(parts[:, :, cut_rows:].transpose(1, 0, 2, 3).reshape(-1, width))
        expand_part = lax.psum_scatter(
            jnp.concatenate(expand_full, 1), ("dp", "mp"), scatter_dimension=0, tiled=True
        )
        project_part = lax.psum_scatter(
            jnp.concatenate(project_full, 0), ("dp", "mp"), scatter_dimension=0, tiled=True
        )
        token, v = lax.psum((both(w_keep, w_send), vec), ("dp", "mp"))
        token = lax.dynamic_index_in_dim(token, core, 0, False).astype(BF)
        mine = [lax.dynamic_index_in_dim(token, sc[1] ^ k, 0, False) for k in range(4)]
    unpacked = unpack(
        sc, mine, [swap(w) for w in mine], v, small, large, hidden, channel_expand.shape[1]
    )
    ges, gps, gel, gpl = unpacked[:4]
    (gtg, gts, gbes, gbps, gbel, gbpl, gcg, gcs, gb1, gb2) = [a.reshape(-1) for a in unpacked[4:]]
    return (
        small_output, large_output, small_input_grad, large_input_grad,
        gtg, gts, ges, gbes, gps, gbps, gel, gbel, gpl, gbpl,
        gcg, gcs, expand_part, gb1, project_part, gb2,
    )


def solution(mesh):
    replicated = P()
    by_channel = P("dp", None, "mp")
    by_patch = P("dp", "mp", None)
    by_row = P(("dp", "mp"), None)
    return jax.shard_map(
        functools.partial(per_device, mesh.shape["dp"]),
        mesh=mesh,
        in_specs=(by_channel, by_channel, P("mp"), P("mp")) + (replicated,) * 14 + (by_patch, by_patch),
        out_specs=(by_patch, by_patch, by_channel, by_channel)
        + (replicated,) * 12
        + (by_row, replicated, by_row, replicated),
        check_vma=False,
    )
```

time: 691 us -> 318 us (0.46)
  waiting for transfers between devices: 308 us -> 65 us
  matrix products: 170 us -> 0 us
  Pallas kernels: 0 us -> 117 us
  starting transfers between devices: 16.8 us -> 76.5 us
  blocking collectives: 50.7 us -> 0 us
  local copies, waits for them, and re-layouts: 77.8 us -> 36.8 us
  other arithmetic: 44.5 us -> 15.4 us
  between operations: 14.7 us -> 1.97 us
    reduce_scatter x2 -> x0, waiting for transfers between devices: 284 us -> none  [the longest x1 142 us: per_device(): lax.psum_scatter(grad_project_full, ('dp', 'mp'), scatter_dimension=0, ti...]
    dot_general x18 -> x0, matrix products: 170 us -> none  [the longest x1 55.8 us: per_device(): jnp.dot(normed_two, channel_expand, preferred_element_type=jnp.float32)]
    pallas_call x0 -> x19, Pallas kernels: none -> 117 us  [the longest x4 74.2 us: channel(): pl.pallas_call(functools.partial(channel_kernel, is_first, is_last), grid...]
    ppermute x0 -> x70, starting transfers between devices: none -> 76.5 us  [the longest x51 72.5 us: across(): return lax.ppermute(values, 'dp', [(i, i ^ mask) for i in pairs])]
    ppermute x0 -> x70, waiting for transfers between devices: none -> 65 us  [the longest x51 60.9 us: across(): return lax.ppermute(values, 'dp', [(i, i ^ mask) for i in pairs])]
    psum x3 -> x0, blocking collectives: 50.7 us -> none  [the longest x1 43.2 us: per_device(): lax.psum((gain_spread, shift_spread, small_grads[0], small_grads[1], smal...]
    psum x1 -> x0, waiting for transfers between devices: 22 us -> none  [per_device(): lax.psum((gain_spread, shift_spread, small_grads[0], small_grads[1], smal...]
    reduce_sum x10 -> x0, other arithmetic: 20.4 us -> none  [the longest x2 5.24 us: token_backward(): grad_expand_bias = jnp.sum(grad_before.astype(jnp.float32), axis=(0, 2))]
  transfers between devices with their start and end apart: 7 -> 70, of which waited for: 4 -> 18; matrix products, arithmetic and copies ran while one was open for 15% -> 11% of each run, Pallas kernels for 0% -> 4%
where the time goes in v1:
time: 318 us; the launch traced here: 313 us
  Pallas kernels  117 us (37%)
  starting transfers between devices  76.5 us (24%)
  waiting for transfers between devices  65 us (20%)
  local copies, waits for them, and re-layouts  36.8 us (12%)
  other arithmetic  15.4 us (5%)
    pallas_call x4, Pallas kernels, channel(): pl.pallas_call(functools.partial(channel_kernel, is_first, is_last), grid...  74.2 us
    ppermute x51, starting transfers between devices, across(): return lax.ppermute(values, 'dp', [(i, i ^ mask) for i in pairs])  72.5 us
    ppermute x51, waiting for transfers between devices, across(): return lax.ppermute(values, 'dp', [(i, i ^ mask) for i in pairs])  60.9 us
    unnamed x180, local copies, waits for them, and re-layouts  16 us
    pallas_call x1, Pallas kernels, back(): pl.pallas_call(back_kernel, grid_spec=pltpu.PrefetchScalarGridSpec(num_sc...  15.5 us
    pallas_call x1, Pallas kernels, front(): pl.pallas_call(front_kernel, grid_spec=pltpu.PrefetchScalarGridSpec(num_s...  13.4 us
    pallas_call x8, other arithmetic, unpack(): pl.pallas_call(unpack_kernel, grid_spec=pltpu.PrefetchScalarGridSpec(num_...  8.39 us
    select_n x4, other arithmetic, whole_images(): return jnp.where(core == 0, keep_first, keep_last)  6.4 us
  transfers between devices with their start and end apart: 70, of which 18 were waited for; matrix products, arithmetic and copies ran while one was open for 11% of the time, Pallas kernels for 4%

profile of v1, /device:TPU:0, one launch (start us, length us, event | category | flops | bytes accessed | tf_op | source)
XLA Modules:
  0.0 313.0 jit_solution(1124852938119933008)
XLA Ops:
  0.7 2.3 constant_dynamic-slice_fusion.2
  12.5 1.6 pad.12.es
  19.2 13.4 %front.1 = (bf16[2,208,768]{2,1,0:T(8,128)(2,1)}, bf16[2,208,768]{2,1,0:T(8,128)(2,1)}, bf16[2,384,768]{2,1,0:T(8,128)(2,1)}, f32[2,384,768]{2,1,0:T(8,128)}, bf...) custom-call(s32[3]{0:T(128)} %pad_add_fusion.sc.refs_0_, ...), custom_call_target="tpu_custom_call" | custom-call | tf_op jit(solution)/shard_map/front/pallas_call | solution.py:146
  32.6 17.7 %channel.4 = (bf16[4,192,768]{2,1,0:T(8,128)(2,1)}, bf16[4,192,768]{2,1,0:T(8,128)(2,1)}, f32[1,768]{1,0:T(1,128)}, f32[1568,768]{1,0:T(8,128)}, f32[1568,768]{1,0:T(8,128)}) custom-call(s32[3]{0:T(128)} %pad_add_fusion.sc.refs_0_, bf16[416,768]{1,0:T(8,128)(2,1)} %bitcast.42, bf16[1152,768]{1,0:T(8,128)(2,1)} %bitcast.33, bf16[416,768]{1,0:T(8,128)(2,1)} %bitcast.46, ...), custom_call_target="tpu_custom_call" | custom-call | flops 11098128384 | bytes 20971520 | tf_op jit(solution)/shard_map/channel/pallas_call | solution.py:290
  50.3 17.7 %channel.5 = (bf16[4,192,768]{2,1,0:T(8,128)(2,1)}, bf16[4,192,768]{2,1,0:T(8,128)(2,1)}, f32[1,768]{1,0:T(1,128)}, f32[1568,768]{1,0:T(8,128)}, f32[1568,768]{1,0:T(8,128)}) custom-call(s32[3]{0:T(128)} %pad_add_fusion.sc.refs_0_, bf16[416,768]{1,0:T(8,128)(2,1)} %bitcast.43, bf16[1152,768]{1,0:T(8,128)(2,1)} %bitcast.34, bf16[416,768]{1,0:T(8,128)(2,1)} %bitcast.47, ...), custom_call_target="tpu_custom_call" | custom-call | flops 11098128384 | bytes 20971520 | tf_op jit(solution)/shard_map/channel/pallas_call | solution.py:290
  68.1 17.8 %channel.6 = (bf16[4,192,768]{2,1,0:T(8,128)(2,1)}, bf16[4,192,768]{2,1,0:T(8,128)(2,1)}, f32[1,768]{1,0:T(1,128)}, f32[1568,768]{1,0:T(8,128)}, f32[1568,768]{1,0:T(8,128)}) custom-call(s32[3]{0:T(128)} %pad_add_fusion.sc.refs_0_, bf16[416,768]{1,0:T(8,128)(2,1)} %bitcast.44, bf16[1152,768]{1,0:T(8,128)(2,1)} %bitcast.35, bf16[416,768]{1,0:T(8,128)(2,1)} %bitcast.48, ...), custom_call_target="tpu_custom_call" | custom-call | flops 11098128384 | bytes 20971520 | tf_op jit(solution)/shard_map/channel/pallas_call | solution.py:290
  85.9 20.9 %channel.7 = (bf16[4,192,768]{2,1,0:T(8,128)(2,1)}, bf16[4,192,768]{2,1,0:T(8,128)(2,1)}, f32[1,768]{1,0:T(1,128)}, bf16[1568,768]{1,0:T(8,128)(2,1)}, bf16[1568,768]{1,0:T(8,128)(2,1)}, /*index=5*/f32[2,768]{1,0:T(2,128)}) custom-call(s32[3]{0:T(128)} %pad_add_fusion.sc.refs_0_, bf16[416,768]{1,0:T(8,128)(2,1)} %bitcast.45, bf16[1152,768]{1,0:T(8,128)(2,1)} %bitcast.36, ...), custom_call_target="tpu_custom_call" | custom-call | flops 11098128384 | bytes 20971520 | tf_op jit(solution)/shard_map/channel/pallas_call | solution.py:290
  106.9 2.0 slice.18
  108.9 2.8 slice.19
  111.7 15.5 %back.1 = (bf16[2,196,384]{2,1,0:T(8,128)(2,1)}, bf16[2,196,384]{2,1,0:T(8,128)(2,1)}, bf16[2,576,384]{2,1,0:T(8,128)(2,1)}, bf16[2,576,384]{2,1,0:T(8,128)(2,1)...) custom-call(s32[3]{0:T(128)} %pad_add_fusion.sc.refs_0_, ...), custom_call_target="tpu_custom_call" | custom-call | tf_op jit(solution)/shard_map/back/pallas_call | solution.py:396
  127.9 1.8 collective-permute-done.9.refs_4_.refs_5_.refs_6_.refs_7_
  131.4 2.7 collective-permute-start.10
  136.0 1.6 collective-permute-start.16
  137.6 1.9 collective-permute-start.14
  142.0 1.7 collective-permute-start.11
  145.1 7.3 %collective-permute-done.11.refs_2_ = bf16[2,112,384]{2,1,0:T(8,128)(2,1)S(1)} collective-permute-done((bf16[2,112,384]{2,1,0:T(8,128)(2,1)S(1)}, bf16[2,112,384]{2,1,0:T(8,128)(2,1)S(1)}, u32[]{:S(2)}, u32[]{:S(2)}) %collective-permute-start.11) | collective-permute-done | bytes 172064 | tf_op jit(solution)/shard_map/ppermute | solution.py:604
  152.5 3.7 %collective-permute-start.19 = (bf16[2,112,384]{2,1,0:T(8,128)(2,1)S(1)}, bf16[2,112,384]{2,1,0:T(8,128)(2,1)S(1)}, u32[]{:S(2)}, u32[]{:S(2)}) collective-permute-start(bf16[2,112,384]{2,1,0:T(8,128)(2,1)S(1)} %get-tuple-element.154.refs_0_), channel_id=1, source_target_pairs={{0,24},{2,26},{4,28},{6,30},{8,16},{10,18},{12,20},{14,22},{16,8},... | collective-permute-start | bytes 516104 | tf_op jit(solution)/shard_map/ppermute | solution.py:604
  156.2 1.9 collective-permute-start.22
  160.6 5.5 %collective-permute-done.22.refs_7_ = f32[16,768]{1,0:T(8,128)S(1)} collective-permute-done((f32[16,768]{1,0:T(8,128)S(1)}, f32[16,768]{1,0:T(8,128)S(1)}, u32[]{:S(2)}, u32[]{:S(2)}) %collective-permute-start.22) | collective-permute-done | bytes 49184 | tf_op jit(solution)/shard_map/ppermute | solution.py:604
  166.2 8.5 %collective-permute-done.21.refs_6_ = f32[16,768]{1,0:T(8,128)S(1)} collective-permute-done((f32[16,768]{1,0:T(8,128)S(1)}, f32[16,768]{1,0:T(8,128)S(1)}, u32[]{:S(2)}, u32[]{:S(2)}) %collective-permute-start.21) | collective-permute-done | bytes 49184 | tf_op jit(solution)/shard_map/ppermute | solution.py:604
  177.4 4.1 %collective-permute-done.17.refs_1_ = bf16[2,112,384]{2,1,0:T(8,128)(2,1)S(1)} collective-permute-done((bf16[2,112,384]{2,1,0:T(8,128)(2,1)S(1)}, bf16[2,112,384]{2,1,0:T(8,128)(2,1)S(1)}, u32[]{:S(2)}, u32[]{:S(2)}) %collective-permute-start.17) | collective-permute-done | bytes 172064 | tf_op jit(solution)/shard_map/ppermute | solution.py:604
  181.7 2.3 collective-permute-done.6
  185.5 2.5 collective-permute-start.24
  189.4 1.6 collective-permute-start.31
  191.1 2.2 collective-permute-done.25.refs_3_
  193.2 3.1 %collective-permute-done.24.refs_2_ = bf16[2,112,384]{2,1,0:T(8,128)(2,1)S(1)} collective-permute-done((bf16[2,112,384]{2,1,0:T(8,128)(2,1)S(1)}, bf16[2,112,384]{2,1,0:T(8,128)(2,1)S(1)}, u32[]{:S(2)}, u32[]{:S(2)}) %collective-permute-start.24) | collective-permute-done | bytes 172064 | tf_op jit(solution)/shard_map/ppermute | solution.py:604
  196.9 1.5 collective-permute-start.33
  202.6 2.2 collective-permute-start.54
  205.2 4.3 %collective-permute-done.33.r3 = bf16[192,768]{1,0:T(8,128)(2,1)S(1)} collective-permute-done((bf16[192,768]{1,0:T(8,128)(2,1)S(1)}, bf16[192,768]{1,0:T(8,128)(2,1)S(1)}, u32[]{:S(2)}, u32[]{:S(2)}) %collective-permute-start.33) | collective-permute-done | bytes 294944 | tf_op jit(solution)/shard_map/ppermute | solution.py:604
  210.5 4.0 %collective-permute-done.52.r1 = bf16[192,768]{1,0:T(8,128)(2,1)S(1)} collective-permute-done((bf16[192,768]{1,0:T(8,128)(2,1)S(1)}, bf16[192,768]{1,0:T(8,128)(2,1)S(1)}, u32[]{:S(2)}, u32[]{:S(2)}) %collective-permute-start.52) | collective-permute-done | bytes 294944 | tf_op jit(solution)/shard_map/ppermute | solution.py:604
  214.5 2.8 collective-permute-start.47
  217.9 4.3 %collective-permute-done.54.r3 = bf16[192,768]{1,0:T(8,128)(2,1)S(1)} collective-permute-done((bf16[192,768]{1,0:T(8,128)(2,1)S(1)}, bf16[192,768]{1,0:T(8,128)(2,1)S(1)}, u32[]{:S(2)}, u32[]{:S(2)}) %collective-permute-start.54) | collective-permute-done | bytes 294944 | tf_op jit(solution)/shard_map/ppermute | solution.py:604
  222.4 4.9 %collective-permute-done.45.r1 = bf16[192,768]{1,0:T(8,128)(2,1)S(1)} collective-permute-done((bf16[192,768]{1,0:T(8,128)(2,1)S(1)}, bf16[192,768]{1,0:T(8,128)(2,1)S(1)}, u32[]{:S(2)}, u32[]{:S(2)}) %collective-permute-start.45) | collective-permute-done | bytes 294944 | tf_op jit(solution)/shard_map/ppermute | solution.py:604
  227.2 2.8 collective-permute-start.40
  234.9 2.3 collective-permute-start.35
  237.3 2.6 collective-permute-done.38.r1
  239.9 2.5 collective-permute-start.36
  242.4 4.6 %collective-permute-done.40.r3 = bf16[192,768]{1,0:T(8,128)(2,1)S(1)} collective-permute-done((bf16[192,768]{1,0:T(8,128)(2,1)S(1)}, bf16[192,768]{1,0:T(8,128)(2,1)S(1)}, u32[]{:S(2)}, u32[]{:S(2)}) %collective-permute-start.40) | collective-permute-done | bytes 294944 | tf_op jit(solution)/shard_map/ppermute | solution.py:604
  247.0 1.5 collective-permute-start.56
  254.8 4.4 %collective-permute-start.49 = (bf16[24,768]{1,0:T(8,128)(2,1)S(1)}, bf16[24,768]{1,0:T(8,128)(2,1)S(1)}, u32[]{:S(2)}, u32[]{:S(2)}) collective-permute-start(bf16[24,768]{1,0:T(8,128)(2,1)S(1)} %get-tuple-element.198), channel_id=1, source_target_pairs={{0,16},{2,18},{4,20},{6,22},{8,24},{10,26},{12,28},{14,30},{16,0},... | collective-permute-start | bytes 110600 | tf_op jit(solution)/shard_map/ppermute | solution.py:604
  263.1 3.8 %collective-permute-done.49.refs_10_ = bf16[24,768]{1,0:T(8,128)(2,1)S(1)} collective-permute-done((bf16[24,768]{1,0:T(8,128)(2,1)S(1)}, bf16[24,768]{1,0:T(8,128)(2,1)S(1)}, u32[]{:S(2)}, u32[]{:S(2)}) %collective-permute-start.49) | collective-permute-done | bytes 36896 | tf_op jit(solution)/shard_map/ppermute | solution.py:604
  267.0 1.9 maximum_select_fusion.3
  271.9 5.1 %collective-permute-start.69 = (bf16[96,768]{1,0:T(8,128)(2,1)S(1)}, bf16[96,768]{1,0:T(8,128)(2,1)S(1)}, u32[]{:S(2)}, u32[]{:S(2)}) collective-permute-start(bf16[96,768]{1,0:T(8,128)(2,1)S(1)} %copy-done.10), channel_id=1, source_target_pairs={{0,24},{2,26},{4,28},{6,30},{1,25},{3,27},{5,29},{7,31}} | collective-permute-start | bytes 442376 | tf_op jit(solution)/shard_map/ppermute | solution.py:604
  279.1 1.5 maximum_select_fusion.1
  280.6 5.0 %collective-permute-start.65 = (bf16[96,768]{1,0:T(8,128)(2,1)}, bf16[96,768]{1,0:T(8,128)(2,1)}, u32[]{:S(2)}, u32[]{:S(2)}) collective-permute-start(bf16[96,768]{1,0:T(8,128)(2,1)} %get-tuple-element.212.refs_24_), channel_id=1, source_target_pairs={{0,16},{2,18},{4,20},{6,22},{1,17},{3,19},{5,21},{7,23}} | collective-permute-start | bytes 442376 | tf_op jit(solution)/shard_map/ppermute | solution.py:604
  289.6 3.1 collective-permute-start.61
  294.3 2.0 unpack.1
  309.9 2.9 last_sum.1
  (331 shorter events, 76.8 us)
Async XLA Ops:
  3.0 14.5 %collective-permute-start.1 = (bf16[2,576,384]{2,1,0:T(8,128)(2,1)}, bf16[2,576,384]{2,1,0:T(8,128)(2,1)}, u32[]{:S(2)}, u32[]{:S(2)}) collective-permute-start(bf16[2,576,384]{2,1,0:T(8,128)(2,1)} %constant_dynamic-slice_fusion.2), channel_id=1, source_target_pairs={{0,1},{1,0},{2,3},{3,2},{4,5},{5,4},{6,7},{7,6},{8,9},{9,8},{10,11... | collective-permute-start | bytes 2654216 | tf_op jit(solution)/shard_map/ppermute | solution.py:600
  4.5 13.0 %collective-permute-start.3 = (bf16[2,288,768]{2,1,0:T(8,128)(2,1)}, bf16[2,288,768]{2,1,0:T(8,128)(2,1)S(1)}, u32[]{:S(2)}, u32[]{:S(2)}) collective-permute-start(bf16[2,288,768]{2,1,0:T(8,128)(2,1)} %constant_dynamic-slice_fusion), channel_id=1, source_target_pairs={{0,1},{1,0},{2,3},{3,2},{4,5},{5,4},{6,7},{7,6},{8,9},{9,8},{10,11... | collective-permute-start | bytes 2654216 | tf_op jit(solution)/shard_map/ppermute | solution.py:600
  5.6 11.9 %collective-permute-start = (bf16[2,196,384]{2,1,0:T(8,128)(2,1)}, bf16[2,196,384]{2,1,0:T(8,128)(2,1)S(1)}, u32[]{:S(2)}, u32[]{:S(2)}) collective-permute-start(bf16[2,196,384]{2,1,0:T(8,128)(2,1)} %constant_dynamic-slice_fusion.3), channel_id=1, source_target_pairs={{0,1},{1,0},{2,3},{3,2},{4,5},{5,4},{6,7},{7,6},{8,9},{9,8},{10,11... | collective-permute-start | bytes 903176 | tf_op jit(solution)/shard_map/ppermute | solution.py:600
  6.9 10.6 %collective-permute-start.2 = (bf16[2,98,768]{2,1,0:T(8,128)(2,1)}, bf16[2,98,768]{2,1,0:T(8,128)(2,1)S(1)}, u32[]{:S(2)}, u32[]{:S(2)}) collective-permute-start(bf16[2,98,768]{2,1,0:T(8,128)(2,1)} %constant_dynamic-slice_fusion.1), channel_id=1, source_target_pairs={{0,1},{1,0},{2,3},{3,2},{4,5},{5,4},{6,7},{7,6},{8,9},{9,8},{10,11... | collective-permute-start | bytes 903176 | tf_op jit(solution)/shard_map/ppermute | solution.py:600
  7.0 10.5 %collective-permute-start.4 = (f32[2,384]{1,0:T(2,128)S(1)}, f32[2,384]{1,0:T(2,128)S(1)}, u32[]{:S(2)}, u32[]{:S(2)}) collective-permute-start(f32[2,384]{1,0:T(2,128)S(1)} %pad_maximum_fusion.tok), channel_id=1, source_target_pairs={{0,1},{1,0},{2,3},{3,2},{4,5},{5,4},{6,7},{7,6},{8,9},{9,8},{10,11... | collective-permute-start | bytes 9224 | tf_op jit(solution)/shard_map/ppermute | solution.py:600
  127.3 31.9 %collective-permute-start.8 = (bf16[2,576,384]{2,1,0:T(8,128)(2,1)}, bf16[2,576,384]{2,1,0:T(8,128)(2,1)S(1)}, u32[]{:S(2)}, u32[]{:S(2)}) collective-permute-start(bf16[2,576,384]{2,1,0:T(8,128)(2,1)} %get-tuple-element.146), channel_id=1, source_target_pairs={{0,1},{1,0},{2,3},{3,2},{4,5},{5,4},{6,7},{7,6},{8,9},{9,8},{10,11... | collective-permute-start | bytes 2654216 | tf_op jit(solution)/shard_map/ppermute | solution.py:600
  131.4 12.2 %collective-permute-start.10 = (bf16[2,112,384]{2,1,0:T(8,128)(2,1)S(1)}, bf16[2,112,384]{2,1,0:T(8,128)(2,1)S(1)}, u32[]{:S(2)}, u32[]{:S(2)}) collective-permute-start(bf16[2,112,384]{2,1,0:T(8,128)(2,1)S(1)} %get-tuple-element.150), channel_id=1, source_target_pairs={{0,2},{2,0},{4,6},{6,4},{8,10},{10,8},{12,14},{14,12},{16,18},{18,... | collective-permute-start | bytes 516104 | tf_op jit(solution)/shard_map/ppermute | solution.py:604
  141.4 14.7 %collective-permute-start.5 = (bf16[2,98,768]{2,1,0:T(8,128)(2,1)S(1)}, bf16[2,98,768]{2,1,0:T(8,128)(2,1)S(1)}, u32[]{:S(2)}, u32[]{:S(2)}) collective-permute-start(bf16[2,98,768]{2,1,0:T(8,128)(2,1)S(1)} %copy.97), channel_id=1, source_target_pairs={{0,1},{1,0},{2,3},{3,2},{4,5},{5,4},{6,7},{7,6},{8,9},{9,8},{10,11... | collective-permute-start | bytes 903176 | tf_op jit(solution)/shard_map/ppermute | solution.py:600
  141.9 16.2 %collective-permute-start.7 = (bf16[2,196,384]{2,1,0:T(8,128)(2,1)S(1)}, bf16[2,196,384]{2,1,0:T(8,128)(2,1)S(1)}, u32[]{:S(2)}, u32[]{:S(2)}) collective-permute-start(bf16[2,196,384]{2,1,0:T(8,128)(2,1)S(1)} %copy-done.85), channel_id=1, source_target_pairs={{0,1},{1,0},{2,3},{3,2},{4,5},{5,4},{6,7},{7,6},{8,9},{9,8},{10,11... | collective-permute-start | bytes 903176 | tf_op jit(solution)/shard_map/ppermute | solution.py:600
  142.0 10.4 %collective-permute-start.11 = (bf16[2,112,384]{2,1,0:T(8,128)(2,1)S(1)}, bf16[2,112,384]{2,1,0:T(8,128)(2,1)S(1)}, u32[]{:S(2)}, u32[]{:S(2)}) collective-permute-start(bf16[2,112,384]{2,1,0:T(8,128)(2,1)S(1)} %get-tuple-element.151), channel_id=1, source_target_pairs={{0,4},{2,6},{4,0},{6,2},{8,12},{10,14},{12,8},{14,10},{16,20},{18,... | collective-permute-start | bytes 516104 | tf_op jit(solution)/shard_map/ppermute | solution.py:604
  152.5 22.7 %collective-permute-start.19 = (bf16[2,112,384]{2,1,0:T(8,128)(2,1)S(1)}, bf16[2,112,384]{2,1,0:T(8,128)(2,1)S(1)}, u32[]{:S(2)}, u32[]{:S(2)}) collective-permute-start(bf16[2,112,384]{2,1,0:T(8,128)(2,1)S(1)} %get-tuple-element.154.refs_0_), channel_id=1, source_target_pairs={{0,24},{2,26},{4,28},{6,30},{8,16},{10,18},{12,20},{14,22},{16,8},... | collective-permute-start | bytes 516104 | tf_op jit(solution)/shard_map/ppermute | solution.py:604
  156.2 19.3 %collective-permute-start.18 = (bf16[2,112,384]{2,1,0:T(8,128)(2,1)S(1)}, bf16[2,112,384]{2,1,0:T(8,128)(2,1)S(1)}, u32[]{:S(2)}, u32[]{:S(2)}) collective-permute-start(bf16[2,112,384]{2,1,0:T(8,128)(2,1)S(1)} %get-tuple-element.154.refs_0_), channel_id=1, source_target_pairs={{0,16},{2,18},{4,20},{6,22},{8,24},{10,26},{12,28},{14,30},{16,0},... | collective-permute-start | bytes 516104 | tf_op jit(solution)/shard_map/ppermute | solution.py:604
  158.1 16.5 %collective-permute-start.21 = (f32[16,768]{1,0:T(8,128)S(1)}, f32[16,768]{1,0:T(8,128)S(1)}, u32[]{:S(2)}, u32[]{:S(2)}) collective-permute-start(f32[16,768]{1,0:T(8,128)S(1)} %get-tuple-element.155.refs_4_), channel_id=1, source_target_pairs={{0,16},{2,18},{4,20},{6,22},{8,24},{10,26},{12,28},{14,30},{16,0},... | collective-permute-start | bytes 147464 | tf_op jit(solution)/shard_map/ppermute | solution.py:604
  159.2 15.4 %collective-permute-start.20 = (f32[16,768]{1,0:T(8,128)S(1)}, f32[16,768]{1,0:T(8,128)S(1)}, u32[]{:S(2)}, u32[]{:S(2)}) collective-permute-start(f32[16,768]{1,0:T(8,128)S(1)} %get-tuple-element.155.refs_4_), channel_id=1, source_target_pairs={{0,8},{2,10},{4,12},{6,14},{8,0},{10,2},{12,4},{14,6},{16,24},{18,... | collective-permute-start | bytes 147464 | tf_op jit(solution)/shard_map/ppermute | solution.py:604
  166.2 18.9 %collective-permute-start.30 = (bf16[4,192,768]{2,1,0:T(8,128)(2,1)S(1)}, bf16[4,192,768]{2,1,0:T(8,128)(2,1)S(1)}, u32[]{:S(2)}, u32[]{:S(2)}) collective-permute-start(bf16[4,192,768]{2,1,0:T(8,128)(2,1)S(1)} %copy-done.83), channel_id=1, source_target_pairs={{0,1},{1,0},{2,3},{3,2},{4,5},{5,4},{6,7},{7,6},{8,9},{9,8},{10,11... | collective-permute-start | bytes 3538952 | tf_op jit(solution)/shard_map/ppermute | solution.py:600
  174.6 10.9 %collective-permute-start.51 = (bf16[4,192,768]{2,1,0:T(8,128)(2,1)S(1)}, bf16[4,192,768]{2,1,0:T(8,128)(2,1)S(1)}, u32[]{:S(2)}, u32[]{:S(2)}) collective-permute-start(bf16[4,192,768]{2,1,0:T(8,128)(2,1)S(1)} %copy-done.82), channel_id=1, source_target_pairs={{0,1},{1,0},{2,3},{3,2},{4,5},{5,4},{6,7},{7,6},{8,9},{9,8},{10,11... | collective-permute-start | bytes 3538952 | tf_op jit(solution)/shard_map/ppermute | solution.py:600
  174.7 13.4 %collective-permute-start.44 = (bf16[4,192,768]{2,1,0:T(8,128)(2,1)S(1)}, bf16[4,192,768]{2,1,0:T(8,128)(2,1)S(1)}, u32[]{:S(2)}, u32[]{:S(2)}) collective-permute-start(bf16[4,192,768]{2,1,0:T(8,128)(2,1)S(1)} %copy-done.84), channel_id=1, source_target_pairs={{0,1},{1,0},{2,3},{3,2},{4,5},{5,4},{6,7},{7,6},{8,9},{9,8},{10,11... | collective-permute-start | bytes 3538952 | tf_op jit(solution)/shard_map/ppermute | solution.py:600
  175.9 13.5 %collective-permute-start.37 = (bf16[4,192,768]{2,1,0:T(8,128)(2,1)S(1)}, bf16[4,192,768]{2,1,0:T(8,128)(2,1)S(1)}, u32[]{:S(2)}, u32[]{:S(2)}) collective-permute-start(bf16[4,192,768]{2,1,0:T(8,128)(2,1)S(1)} %copy-done.81), channel_id=1, source_target_pairs={{0,1},{1,0},{2,3},{3,2},{4,5},{5,4},{6,7},{7,6},{8,9},{9,8},{10,11... | collective-permute-start | bytes 3538952 | tf_op jit(solution)/shard_map/ppermute | solution.py:600
  185.5 10.8 %collective-permute-start.24 = (bf16[2,112,384]{2,1,0:T(8,128)(2,1)S(1)}, bf16[2,112,384]{2,1,0:T(8,128)(2,1)S(1)}, u32[]{:S(2)}, u32[]{:S(2)}) collective-permute-start(bf16[2,112,384]{2,1,0:T(8,128)(2,1)S(1)} %get-tuple-element.156.refs_0_), channel_id=1, source_target_pairs={{0,4},{2,6},{4,0},{6,2},{8,12},{10,14},{12,8},{14,10},{16,20},{18,... | collective-permute-start | bytes 516104 | tf_op jit(solution)/shard_map/ppermute | solution.py:604
  189.4 13.1 %collective-permute-start.31 = (bf16[192,768]{1,0:T(8,128)(2,1)S(1)}, bf16[192,768]{1,0:T(8,128)(2,1)S(1)}, u32[]{:S(2)}, u32[]{:S(2)}) collective-permute-start(bf16[192,768]{1,0:T(8,128)(2,1)S(1)} %get-tuple-element.173), channel_id=1, source_target_pairs={{0,2},{2,0},{4,6},{6,4},{8,10},{10,8},{12,14},{14,12},{16,18},{18,... | collective-permute-start | bytes 884744 | tf_op jit(solution)/shard_map/ppermute | solution.py:604
  191.0 13.7 %collective-permute-start.32 = (bf16[192,768]{1,0:T(8,128)(2,1)S(1)}, bf16[192,768]{1,0:T(8,128)(2,1)S(1)}, u32[]{:S(2)}, u32[]{:S(2)}) collective-permute-start(bf16[192,768]{1,0:T(8,128)(2,1)S(1)} %get-tuple-element.174), channel_id=1, source_target_pairs={{0,4},{2,6},{4,0},{6,2},{8,12},{10,14},{12,8},{14,10},{16,20},{18,... | collective-permute-start | bytes 884744 | tf_op jit(solution)/shard_map/ppermute | solution.py:604
  196.9 12.7 %collective-permute-start.33 = (bf16[192,768]{1,0:T(8,128)(2,1)S(1)}, bf16[192,768]{1,0:T(8,128)(2,1)S(1)}, u32[]{:S(2)}, u32[]{:S(2)}) collective-permute-start(bf16[192,768]{1,0:T(8,128)(2,1)S(1)} %get-tuple-element.175), channel_id=1, source_target_pairs={{0,6},{2,4},{4,2},{6,0},{8,14},{10,12},{12,10},{14,8},{16,22},{18,... | collective-permute-start | bytes 884744 | tf_op jit(solution)/shard_map/ppermute | solution.py:604
  200.5 14.0 %collective-permute-start.52 = (bf16[192,768]{1,0:T(8,128)(2,1)S(1)}, bf16[192,768]{1,0:T(8,128)(2,1)S(1)}, u32[]{:S(2)}, u32[]{:S(2)}) collective-permute-start(bf16[192,768]{1,0:T(8,128)(2,1)S(1)} %get-tuple-element.203), channel_id=1, source_target_pairs={{0,2},{2,0},{4,6},{6,4},{8,10},{10,8},{12,14},{14,12},{16,18},{18,... | collective-permute-start | bytes 884744 | tf_op jit(solution)/shard_map/ppermute | solution.py:604
  201.1 16.3 %collective-permute-start.53 = (bf16[192,768]{1,0:T(8,128)(2,1)S(1)}, bf16[192,768]{1,0:T(8,128)(2,1)S(1)}, u32[]{:S(2)}, u32[]{:S(2)}) collective-permute-start(bf16[192,768]{1,0:T(8,128)(2,1)S(1)} %get-tuple-element.204), channel_id=1, source_target_pairs={{0,4},{2,6},{4,0},{6,2},{8,12},{10,14},{12,8},{14,10},{16,20},{18,... | collective-permute-start | bytes 884744 | tf_op jit(solution)/shard_map/ppermute | solution.py:604
  202.6 19.7 %collective-permute-start.54 = (bf16[192,768]{1,0:T(8,128)(2,1)S(1)}, bf16[192,768]{1,0:T(8,128)(2,1)S(1)}, u32[]{:S(2)}, u32[]{:S(2)}) collective-permute-start(bf16[192,768]{1,0:T(8,128)(2,1)S(1)} %get-tuple-element.205), channel_id=1, source_target_pairs={{0,6},{2,4},{4,2},{6,0},{8,14},{10,12},{12,10},{14,8},{16,22},{18,... | collective-permute-start | bytes 884744 | tf_op jit(solution)/shard_map/ppermute | solution.py:604
  204.7 22.5 %collective-permute-start.45 = (bf16[192,768]{1,0:T(8,128)(2,1)S(1)}, bf16[192,768]{1,0:T(8,128)(2,1)S(1)}, u32[]{:S(2)}, u32[]{:S(2)}) collective-permute-start(bf16[192,768]{1,0:T(8,128)(2,1)S(1)} %get-tuple-element.193), channel_id=1, source_target_pairs={{0,2},{2,0},{4,6},{6,4},{8,10},{10,8},{12,14},{14,12},{16,18},{18,... | collective-permute-start | bytes 884744 | tf_op jit(solution)/shard_map/ppermute | solution.py:604
  209.6 21.9 %collective-permute-start.46 = (bf16[192,768]{1,0:T(8,128)(2,1)S(1)}, bf16[192,768]{1,0:T(8,128)(2,1)S(1)}, u32[]{:S(2)}, u32[]{:S(2)}) collective-permute-start(bf16[192,768]{1,0:T(8,128)(2,1)S(1)} %get-tuple-element.194), channel_id=1, source_target_pairs={{0,4},{2,6},{4,0},{6,2},{8,12},{10,14},{12,8},{14,10},{16,20},{18,... | collective-permute-start | bytes 884744 | tf_op jit(solution)/shard_map/ppermute | solution.py:604
  214.5 20.4 %collective-permute-start.47 = (bf16[192,768]{1,0:T(8,128)(2,1)S(1)}, bf16[192,768]{1,0:T(8,128)(2,1)S(1)}, u32[]{:S(2)}, u32[]{:S(2)}) collective-permute-start(bf16[192,768]{1,0:T(8,128)(2,1)S(1)} %get-tuple-element.195), channel_id=1, source_target_pairs={{0,6},{2,4},{4,2},{6,0},{8,14},{10,12},{12,10},{14,8},{16,22},{18,... | collective-permute-start | bytes 884744 | tf_op jit(solution)/shard_map/ppermute | solution.py:604
  217.4 22.5 %collective-permute-start.38 = (bf16[192,768]{1,0:T(8,128)(2,1)S(1)}, bf16[192,768]{1,0:T(8,128)(2,1)S(1)}, u32[]{:S(2)}, u32[]{:S(2)}) collective-permute-start(bf16[192,768]{1,0:T(8,128)(2,1)S(1)} %get-tuple-element.183), channel_id=1, source_target_pairs={{0,2},{2,0},{4,6},{6,4},{8,10},{10,8},{12,14},{14,12},{16,18},{18,... | collective-permute-start | bytes 884744 | tf_op jit(solution)/shard_map/ppermute | solution.py:604
  222.3 20.1 %collective-permute-start.39 = (bf16[192,768]{1,0:T(8,128)(2,1)S(1)}, bf16[192,768]{1,0:T(8,128)(2,1)S(1)}, u32[]{:S(2)}, u32[]{:S(2)}) collective-permute-start(bf16[192,768]{1,0:T(8,128)(2,1)S(1)} %get-tuple-element.184), channel_id=1, source_target_pairs={{0,4},{2,6},{4,0},{6,2},{8,12},{10,14},{12,8},{14,10},{16,20},{18,... | collective-permute-start | bytes 884744 | tf_op jit(solution)/shard_map/ppermute | solution.py:604
  227.2 19.8 %collective-permute-start.40 = (bf16[192,768]{1,0:T(8,128)(2,1)S(1)}, bf16[192,768]{1,0:T(8,128)(2,1)S(1)}, u32[]{:S(2)}, u32[]{:S(2)}) collective-permute-start(bf16[192,768]{1,0:T(8,128)(2,1)S(1)} %get-tuple-element.185), channel_id=1, source_target_pairs={{0,6},{2,4},{4,2},{6,0},{8,14},{10,12},{12,10},{14,8},{16,22},{18,... | collective-permute-start | bytes 884744 | tf_op jit(solution)/shard_map/ppermute | solution.py:604
  231.5 17.0 %collective-permute-start.34 = (bf16[24,768]{1,0:T(8,128)(2,1)S(1)}, bf16[24,768]{1,0:T(8,128)(2,1)S(1)}, u32[]{:S(2)}, u32[]{:S(2)}) collective-permute-start(bf16[24,768]{1,0:T(8,128)(2,1)S(1)} %get-tuple-element.177), channel_id=1, source_target_pairs={{0,8},{2,10},{4,12},{6,14},{8,0},{10,2},{12,4},{14,6},{16,24},{18,... | collective-permute-start | bytes 110600 | tf_op jit(solution)/shard_map/ppermute | solution.py:604
  234.9 17.0 %collective-permute-start.35 = (bf16[24,768]{1,0:T(8,128)(2,1)}, bf16[24,768]{1,0:T(8,128)(2,1)}, u32[]{:S(2)}, u32[]{:S(2)}) collective-permute-start(bf16[24,768]{1,0:T(8,128)(2,1)} %get-tuple-element.178), channel_id=1, source_target_pairs={{0,16},{2,18},{4,20},{6,22},{8,24},{10,26},{12,28},{14,30},{16,0},... | collective-permute-start | bytes 110600 | tf_op jit(solution)/shard_map/ppermute | solution.py:604
  239.9 13.5 %collective-permute-start.36 = (bf16[24,768]{1,0:T(8,128)(2,1)}, bf16[24,768]{1,0:T(8,128)(2,1)}, u32[]{:S(2)}, u32[]{:S(2)}) collective-permute-start(bf16[24,768]{1,0:T(8,128)(2,1)} %get-tuple-element.179), channel_id=1, source_target_pairs={{0,24},{2,26},{4,28},{6,30},{8,16},{10,18},{12,20},{14,22},{16,8},... | collective-permute-start | bytes 110600 | tf_op jit(solution)/shard_map/ppermute | solution.py:604
  242.4 12.3 %collective-permute-start.55 = (bf16[24,768]{1,0:T(8,128)(2,1)}, bf16[24,768]{1,0:T(8,128)(2,1)}, u32[]{:S(2)}, u32[]{:S(2)}) collective-permute-start(bf16[24,768]{1,0:T(8,128)(2,1)} %get-tuple-element.207), channel_id=1, source_target_pairs={{0,8},{2,10},{4,12},{6,14},{8,0},{10,2},{12,4},{14,6},{16,24},{18,... | collective-permute-start | bytes 110600 | tf_op jit(solution)/shard_map/ppermute | solution.py:604
  252.0 25.7 %collective-permute-start.60 = (bf16[96,768]{1,0:T(8,128)(2,1)S(1)}, bf16[96,768]{1,0:T(8,128)(2,1)S(1)}, u32[]{:S(2)}, u32[]{:S(2)}) collective-permute-start(bf16[96,768]{1,0:T(8,128)(2,1)S(1)} %get-tuple-element.210.refs_16_), channel_id=1, source_target_pairs={{24,0},{26,2},{28,4},{30,6},{25,1},{27,3},{29,5},{31,7}} | collective-permute-start | bytes 442376 | tf_op jit(solution)/shard_map/ppermute | solution.py:604
  253.4 25.0 %collective-permute-start.59 = (bf16[96,768]{1,0:T(8,128)(2,1)S(1)}, bf16[96,768]{1,0:T(8,128)(2,1)S(1)}, u32[]{:S(2)}, u32[]{:S(2)}) collective-permute-start(bf16[96,768]{1,0:T(8,128)(2,1)S(1)} %get-tuple-element.210.refs_16_), channel_id=1, source_target_pairs={{16,0},{18,2},{20,4},{22,6},{17,1},{19,3},{21,5},{23,7}} | collective-permute-start | bytes 442376 | tf_op jit(solution)/shard_map/ppermute | solution.py:604
  254.8 12.1 %collective-permute-start.49 = (bf16[24,768]{1,0:T(8,128)(2,1)S(1)}, bf16[24,768]{1,0:T(8,128)(2,1)S(1)}, u32[]{:S(2)}, u32[]{:S(2)}) collective-permute-start(bf16[24,768]{1,0:T(8,128)(2,1)S(1)} %get-tuple-element.198), channel_id=1, source_target_pairs={{0,16},{2,18},{4,20},{6,22},{8,24},{10,26},{12,28},{14,30},{16,0},... | collective-permute-start | bytes 110600 | tf_op jit(solution)/shard_map/ppermute | solution.py:604
  266.9 10.1 %collective-permute-start.43 = (bf16[24,768]{1,0:T(8,128)(2,1)S(1)}, bf16[24,768]{1,0:T(8,128)(2,1)S(1)}, u32[]{:S(2)}, u32[]{:S(2)}) collective-permute-start(bf16[24,768]{1,0:T(8,128)(2,1)S(1)} %get-tuple-element.189), channel_id=1, source_target_pairs={{0,24},{2,26},{4,28},{6,30},{8,16},{10,18},{12,20},{14,22},{16,8},... | collective-permute-start | bytes 110600 | tf_op jit(solution)/shard_map/ppermute | solution.py:604
  270.6 10.1 %collective-permute-start.58 = (bf16[96,768]{1,0:T(8,128)(2,1)S(1)}, bf16[96,768]{1,0:T(8,128)(2,1)S(1)}, u32[]{:S(2)}, u32[]{:S(2)}) collective-permute-start(bf16[96,768]{1,0:T(8,128)(2,1)S(1)} %get-tuple-element.210.refs_16_), channel_id=1, source_target_pairs={{8,0},{10,2},{12,4},{14,6},{9,1},{11,3},{13,5},{15,7}} | collective-permute-start | bytes 442376 | tf_op jit(solution)/shard_map/ppermute | solution.py:604
  271.9 13.8 %collective-permute-start.69 = (bf16[96,768]{1,0:T(8,128)(2,1)S(1)}, bf16[96,768]{1,0:T(8,128)(2,1)S(1)}, u32[]{:S(2)}, u32[]{:S(2)}) collective-permute-start(bf16[96,768]{1,0:T(8,128)(2,1)S(1)} %copy-done.10), channel_id=1, source_target_pairs={{0,24},{2,26},{4,28},{6,30},{1,25},{3,27},{5,29},{7,31}} | collective-permute-start | bytes 442376 | tf_op jit(solution)/shard_map/ppermute | solution.py:604
  277.7 10.6 %collective-permute-start.67 = (bf16[96,768]{1,0:T(8,128)(2,1)S(1)}, bf16[96,768]{1,0:T(8,128)(2,1)S(1)}, u32[]{:S(2)}, u32[]{:S(2)}) collective-permute-start(bf16[96,768]{1,0:T(8,128)(2,1)S(1)} %copy-done.10), channel_id=1, source_target_pairs={{16,24},{18,26},{20,28},{22,30},{17,25},{19,27},{21,29},{23,31}} | collective-permute-start | bytes 442376 | tf_op jit(solution)/shard_map/ppermute | solution.py:604
  278.4 11.2 %collective-permute-start.66 = (bf16[96,768]{1,0:T(8,128)(2,1)}, bf16[96,768]{1,0:T(8,128)(2,1)S(1)}, u32[]{:S(2)}, u32[]{:S(2)}) collective-permute-start(bf16[96,768]{1,0:T(8,128)(2,1)} %get-tuple-element.212.refs_24_), channel_id=1, source_target_pairs={{8,16},{10,18},{12,20},{14,22},{9,17},{11,19},{13,21},{15,23}} | collective-permute-start | bytes 442376 | tf_op jit(solution)/shard_map/ppermute | solution.py:604
  280.6 29.1 %collective-permute-start.65 = (bf16[96,768]{1,0:T(8,128)(2,1)}, bf16[96,768]{1,0:T(8,128)(2,1)}, u32[]{:S(2)}, u32[]{:S(2)}) collective-permute-start(bf16[96,768]{1,0:T(8,128)(2,1)} %get-tuple-element.212.refs_24_), channel_id=1, source_target_pairs={{0,16},{2,18},{4,20},{6,22},{1,17},{3,19},{5,21},{7,23}} | collective-permute-start | bytes 442376 | tf_op jit(solution)/shard_map/ppermute | solution.py:604
  285.6 24.1 %collective-permute-start.64 = (bf16[96,768]{1,0:T(8,128)(2,1)}, bf16[96,768]{1,0:T(8,128)(2,1)}, u32[]{:S(2)}, u32[]{:S(2)}) collective-permute-start(bf16[96,768]{1,0:T(8,128)(2,1)} %get-tuple-element.212.refs_24_), channel_id=1, source_target_pairs={{24,16},{26,18},{28,20},{30,22},{25,17},{27,19},{29,21},{31,23}} | collective-permute-start | bytes 442376 | tf_op jit(solution)/shard_map/ppermute | solution.py:604
  287.0 22.8 %collective-permute-start.63 = (bf16[96,768]{1,0:T(8,128)(2,1)S(1)}, bf16[96,768]{1,0:T(8,128)(2,1)}, u32[]{:S(2)}, u32[]{:S(2)}) collective-permute-start(bf16[96,768]{1,0:T(8,128)(2,1)S(1)} %get-tuple-element.211.refs_20_), channel_id=1, source_target_pairs={{16,8},{18,10},{20,12},{22,14},{17,9},{19,11},{21,13},{23,15}} | collective-permute-start | bytes 442376 | tf_op jit(solution)/shard_map/ppermute | solution.py:604
  288.3 21.5 %collective-permute-start.62 = (bf16[96,768]{1,0:T(8,128)(2,1)S(1)}, bf16[96,768]{1,0:T(8,128)(2,1)}, u32[]{:S(2)}, u32[]{:S(2)}) collective-permute-start(bf16[96,768]{1,0:T(8,128)(2,1)S(1)} %get-tuple-element.211.refs_20_), channel_id=1, source_target_pairs={{24,8},{26,10},{28,12},{30,14},{25,9},{27,11},{29,13},{31,15}} | collective-permute-start | bytes 442376 | tf_op jit(solution)/shard_map/ppermute | solution.py:604
  289.6 20.1 %collective-permute-start.61 = (bf16[96,768]{1,0:T(8,128)(2,1)S(1)}, bf16[96,768]{1,0:T(8,128)(2,1)}, u32[]{:S(2)}, u32[]{:S(2)}) collective-permute-start(bf16[96,768]{1,0:T(8,128)(2,1)S(1)} %get-tuple-element.211.refs_20_), channel_id=1, source_target_pairs={{0,8},{2,10},{4,12},{6,14},{1,9},{3,11},{5,13},{7,15}} | collective-permute-start | bytes 442376 | tf_op jit(solution)/shard_map/ppermute | solution.py:604
  (108 other events, 935.8 us)
